TPU v7x, 256 devices: a whole 4x4x8 slice. The times are simulated.
256 devices in a mesh: wide: 32 (over y, x, core), narrow: 8 (over z).
Axes of the slice: x: 4, y: 4, z: 8, core: 2. Of those that a mesh axis runs over, the one named last changes fastest.
Arguments:
- panel: float32 [64, 4194304], P(None, ('wide', 'narrow'))
- signs: int32 [4194304], P(('wide', 'narrow')), may hold values from -1 to 1, as said below
- sample_rows: int32 [16384], replicated, may hold values from 0 to 4194303, as said below
Outputs:
- mixed: float32 [64, 4194304], P(None, ('wide', 'narrow'))
- r_factor: float32 [64, 64], replicated
- precond: float32 [64, 4194304], P(None, ('wide', 'narrow'))
Inputs may be any that keep to these rules, and one draw needn't show every extreme that they name: `signs`: each value is 1 or -1. `sample_rows`: increasing, all distinct.
All inputs are finite; a program needn't handle non-finite values.
Results may differ from a plain program's by a relative error of at most 0.00011.
Values sent between devices are 32-bit elements; how exact they have to be, the bound alone decides.
A program may use at most 64 MiB of HBM per device.

v0:
```python
import math

import jax
import jax.numpy as jnp
from jax import lax
from jax.sharding import PartitionSpec as P


def swapped(block, axis, bit):
    count = lax.axis_size(axis)
    route = []
    for low in range(count):
        high = low | 1 << bit
        if high != low and high < count:
            route += [(low, high), (high, low)]
    return lax.ppermute(block, axis, route)


def sylvester(order):
    matrix = jnp.ones((1, 1), jnp.float32)
    while matrix.shape[0] < order:
        matrix = jnp.concatenate(
            [jnp.concatenate([matrix, matrix], 1), jnp.concatenate([matrix, -matrix], 1)], 0
        )
    return matrix


def local_mix(values):
    cols, count = values.shape
    inner = 128
    outer = count // inner
    blocks = values.reshape(cols, outer, inner)
    blocks = jnp.einsum(
        "kpq,qs->kps",
        blocks,
        sylvester(inner),
        precision=lax.Precision.HIGHEST,
        preferred_element_type=jnp.float32,
    )
    blocks = jnp.einsum(
        "lrm,rf->lfm",
        blocks,
        sylvester(outer),
        precision=lax.Precision.HIGHEST,
        preferred_element_type=jnp.float32,
    )
    return blocks.reshape(cols, count)


def cholesky_lower(gram):
    cols = gram.shape[0]
    places = jnp.arange(cols)
    lower = jnp.zeros((cols, cols), jnp.float32)
    for column in range(cols):
        partial_col = gram[:, column] - jnp.dot(
            lower,
            lower[column, :],
            precision=lax.Precision.HIGHEST,
            preferred_element_type=jnp.float32,
        )
        pivot = jnp.sqrt(partial_col[column])
        filled = jnp.where(
            places > column, partial_col / pivot, jnp.where(places == column, pivot, 0.0)
        )
        lower = lower.at[:, column].set(filled)
    return lower


def lower_inverse(lower):
    cols = lower.shape[0]
    result = jnp.zeros((cols, cols), jnp.float32)
    for line in range(cols):
        unit_row = (jnp.arange(cols) == line).astype(jnp.float32)
        known = jnp.dot(
            lower[line, :],
            result,
            precision=lax.Precision.HIGHEST,
            preferred_element_type=jnp.float32,
        )
        result = result.at[line, :].set((unit_row - known) / lower[line, line])
    return result


def body(panel, signs, sample_rows):
    cols, count = panel.shape
    n_wide = lax.axis_size("wide")
    n_narrow = lax.axis_size("narrow")
    total = count * n_wide * n_narrow
    values = local_mix(panel * signs.astype(jnp.float32)[None, :])
    shaped = values.reshape(cols, n_narrow, count // n_narrow)
    turned = jnp.einsum(
        "ksr,su->kur",
        lax.all_to_all(shaped, "narrow", split_axis=1, concat_axis=1, tiled=True),
        sylvester(n_narrow),
        precision=lax.Precision.HIGHEST,
        preferred_element_type=jnp.float32,
    )
    shaped = lax.all_to_all(turned, "narrow", split_axis=1, concat_axis=1, tiled=True)
    values = shaped.reshape(cols, count)
    for bit in range(n_wide.bit_length() - 1):
        other = swapped(values, "wide", bit)
        upper = jnp.bitwise_and(jnp.right_shift(lax.axis_index("wide"), bit), 1)
        values = jnp.where(upper == 1, other - values, values + other)
    mixed = values * (1.0 / math.sqrt(total))
    base = (lax.axis_index("wide") * n_narrow + lax.axis_index("narrow")) * count
    offsets = sample_rows - base
    inside = (offsets >= 0) & (offsets < count)
    offsets = jnp.where(inside, offsets, count)
    weight = jnp.zeros((count,), jnp.float32).at[offsets].add(1.0, mode="drop")
    share = jnp.dot(
        mixed * weight[None, :],
        mixed.T,
        precision=lax.Precision.HIGHEST,
        preferred_element_type=jnp.float32,
    )
    gram = lax.psum(share, ("wide", "narrow"))
    gram = gram * (total / sample_rows.shape[0])
    lower = cholesky_lower(gram)
    r_factor = lower.T * (1.0 / math.sqrt(total))
    rinv = lower_inverse(lower).T * math.sqrt(total)
    precond = jnp.dot(
        rinv.T, panel, precision=lax.Precision.HIGHEST, preferred_element_type=jnp.float32
    )
    return (mixed, r_factor, precond)


def solution(mesh):
    in_specs = (P(None, ("wide", "narrow")), P(("wide", "narrow")), P())
    out_specs = (P(None, ("wide", "narrow")), P(), P(None, ("wide", "narrow")))
    return jax.shard_map(body, mesh=mesh, in_specs=in_specs, out_specs=out_specs, check_vma=False)
```

profile of v0, /device:TPU:1, one launch (start us, length us, event | category | flops | bytes accessed | tf_op | source)
XLA Modules:
  0.0 975.4 jit_solution(8375361389191867202)
XLA Ops:
  0.6 0.8 convert_element_type.195
  1.5 2.5 multiply_bitcast_fusion
  4.8 3.4 fusion.412
  8.2 5.2 convolution_bitcast_fusion
  13.4 4.9 reshape_reshape.3
  18.3 4.6 copy.11
  22.9 103.6 %all_to_all.10 = f32[64,8,2048]{2,0,1:T(8,128)S(1)} all-to-all(f32[64,8,2048]{2,0,1:T(8,128)S(1)} %copy.11), channel_id=1, replica_groups=mesh['wide'=32,'narrow'=8] {'narrow'}, dimensions={1} | all-to-all | bytes 8388608 | tf_op jit(solution)/shard_map/all_to_all | solution.py:93
  126.6 5.8 fusion.4
  132.4 2.4 copy.13
  134.8 95.6 %all_to_all.11 = f32[64,8,2048]{2,0,1:T(8,128)S(1)} all-to-all(f32[64,8,2048]{2,0,1:T(8,128)S(1)} %copy.13), channel_id=1, replica_groups=mesh['wide'=32,'narrow'=8] {'narrow'}, dimensions={1} | all-to-all | bytes 8388608 | tf_op jit(solution)/shard_map/all_to_all | solution.py:98
  230.4 2.3 copy.17
  232.7 4.0 collective-permute-start
  236.7 7.1 collective-permute-done
  243.8 5.9 add_select_fusion.4
  249.8 1.2 collective-permute-start.1
  251.0 90.9 %collective-permute-done.1 = f32[64,16384]{1,0:T(8,128)} collective-permute-done((f32[64,16384]{1,0:T(8,128)}, f32[64,16384]{1,0:T(8,128)}, u32[]{:S(2)}, u32[]{:S(2)}) %collective-permute-start.1) | collective-permute-done | bytes 4194336 | tf_op jit(solution)/shard_map/ppermute | solution.py:16
  341.9 5.9 add_select_fusion.3
  347.8 2.9 collective-permute-start.2
  350.7 90.0 %collective-permute-done.2 = f32[64,16384]{1,0:T(8,128)} collective-permute-done((f32[64,16384]{1,0:T(8,128)}, f32[64,16384]{1,0:T(8,128)}, u32[]{:S(2)}, u32[]{:S(2)}) %collective-permute-start.2) | collective-permute-done | bytes 4194336 | tf_op jit(solution)/shard_map/ppermute | solution.py:16
  440.7 5.9 add_select_fusion.2
  446.6 1.3 collective-permute-start.3
  447.9 89.0 %collective-permute-done.3 = f32[64,16384]{1,0:T(8,128)} collective-permute-done((f32[64,16384]{1,0:T(8,128)}, f32[64,16384]{1,0:T(8,128)}, u32[]{:S(2)}, u32[]{:S(2)}) %collective-permute-start.3) | collective-permute-done | bytes 4194336 | tf_op jit(solution)/shard_map/ppermute | solution.py:16
  536.8 5.9 add_select_fusion.1
  542.8 2.9 collective-permute-start.4
  545.7 85.8 %scatter_custom_fusion = f32[16384]{0:T(1024)S(1)} fusion(s32[16384]{0:T(1024)S(1)} %compare_select_fusion, f32[16384]{0:T(1024)S(1)} %broadcast.2141, f32[]{:T(128)} %constant.3367.clone.1), kind=kCustom, calls=%fused_computation.595 | custom fusion | flops 16384 | bytes 65540 | tf_op jit(solution)/shard_map/scatter-add | solution.py:109
  673.9 4.0 broadcast_multiply_fusion
  678.0 2.0 copy-done
  680.0 6.5 fusion.2
  686.5 76.5 %psum.7 = f32[64,64]{1,0:T(8,128)S(1)} all-reduce(f32[64,64]{1,0:T(8,128)S(1)} %fusion.2), channel_id=1, replica_groups=mesh['wide'=32,'narrow'=8] {'wide','narrow'}, use_global_device_ids=true, to_apply=%region_2.3 | all-reduce | flops 4096 | bytes 32768 | tf_op jit(solution)/shard_map/psum | solution.py:116
  917.8 0.8 fusion.141
  923.3 0.8 fusion.155
  924.2 0.8 fusion.157
  928.0 0.8 fusion.167
  928.8 0.8 fusion.169
  930.4 0.8 fusion.173
  932.2 0.8 fusion.177
  934.6 0.8 fusion.183
  936.1 0.8 fusion.187
  938.6 0.8 fusion.193
  939.4 0.8 fusion.195
  941.0 0.8 fusion.199
  945.1 0.8 fusion.209
  946.7 0.8 fusion.213
  952.2 0.8 fusion.227
  955.4 0.8 fusion.235
  958.5 0.8 fusion.243
  964.0 0.8 fusion.257
  967.3 7.9 fusion.264
  (519 shorter events, 188.0 us)
Async XLA Ops:
  4.0 0.8 copy-start.1
  22.9 103.6 %copy-start.3 = (f32[8,8,1]{0,1,2:T(8,128)S(1)}, f32[8,8,1]{0,1,2:T(8,128)}, u32[]{:S(2)}) copy-start(f32[8,8,1]{0,1,2:T(8,128)} %constant.3435) | copy-start | bytes 772
  232.7 11.1 %collective-permute-start = (f32[64,16384]{1,0:T(8,128)}, f32[64,16384]{1,0:T(8,128)}, u32[]{:S(2)}, u32[]{:S(2)}) collective-permute-start(f32[64,16384]{1,0:T(8,128)} %bitcast.518), channel_id=1, source_target_pairs={{0,8},{8,0},{16,24},{24,16},{32,40},{40,32},{48,56},{56,48},{64,72... | collective-permute-start | bytes 12582920 | tf_op jit(solution)/shard_map/ppermute | solution.py:16
  249.8 92.1 %collective-permute-start.1 = (f32[64,16384]{1,0:T(8,128)}, f32[64,16384]{1,0:T(8,128)}, u32[]{:S(2)}, u32[]{:S(2)}) collective-permute-start(f32[64,16384]{1,0:T(8,128)} %add_select_fusion.4), channel_id=1, source_target_pairs={{0,16},{16,0},{8,24},{24,8},{32,48},{48,32},{40,56},{56,40},{64,80... | collective-permute-start | bytes 12582920 | tf_op jit(solution)/shard_map/ppermute | solution.py:16
  347.8 92.9 %collective-permute-start.2 = (f32[64,16384]{1,0:T(8,128)}, f32[64,16384]{1,0:T(8,128)}, u32[]{:S(2)}, u32[]{:S(2)}) collective-permute-start(f32[64,16384]{1,0:T(8,128)} %add_select_fusion.3), channel_id=1, source_target_pairs={{0,32},{32,0},{8,40},{40,8},{16,48},{48,16},{24,56},{56,24},{64,96... | collective-permute-start | bytes 12582920 | tf_op jit(solution)/shard_map/ppermute | solution.py:16
  446.6 90.3 %collective-permute-start.3 = (f32[64,16384]{1,0:T(8,128)}, f32[64,16384]{1,0:T(8,128)}, u32[]{:S(2)}, u32[]{:S(2)}) collective-permute-start(f32[64,16384]{1,0:T(8,128)} %add_select_fusion.2), channel_id=1, source_target_pairs={{0,64},{64,0},{8,72},{72,8},{16,80},{80,16},{24,88},{88,24},{32,96... | collective-permute-start | bytes 12582920 | tf_op jit(solution)/shard_map/ppermute | solution.py:16
  447.9 97.8 %copy-start.2 = (s32[16384]{0:T(1024)S(1)}, s32[16384]{0:T(1024)}, u32[]{:S(2)}) copy-start(s32[16384]{0:T(1024)} %param.261) | copy-start | bytes 196612
  542.8 131.2 %collective-permute-start.4 = (f32[64,16384]{1,0:T(8,128)}, f32[64,16384]{1,0:T(8,128)}, u32[]{:S(2)}, u32[]{:S(2)}) collective-permute-start(f32[64,16384]{1,0:T(8,128)} %add_select_fusion.1), channel_id=1, source_target_pairs={{0,128},{128,0},{8,136},{136,8},{16,144},{144,16},{24,152},{152,24... | collective-permute-start | bytes 12582920 | tf_op jit(solution)/shard_map/ppermute | solution.py:16
  677.9 2.0 copy-start
where the time goes:
time: 984 us; the launch traced here: 975 us
  waiting for transfers between devices  277 us (28%)
  blocking collectives  276 us (28%)
  other arithmetic  200 us (20%)
  matrix products  87.1 us (9%)
  local copies, waits for them, and re-layouts  78 us (8%)
  between operations  45.7 us (5%)
  starting transfers between devices  12.3 us (1%)
    ppermute x5, waiting for transfers between devices, swapped(): return lax.ppermute(block, axis, route)  277 us
    all_to_all x1, blocking collectives, body(): lax.all_to_all(shaped, 'narrow', split_axis=1, concat_axis=1, tiled=True)  104 us
    all_to_all x1, blocking collectives, body(): lax.all_to_all(turned, 'narrow', split_axis=1, concat_axis=1, tiled=True)  95.6 us
    scatter-add x1, other arithmetic, body(): weight = jnp.zeros((count,), jnp.float32).at[offsets].add(1.0, mode='drop')  85.8 us
    another operation x127, other arithmetic  82 us
    psum x1, blocking collectives, body(): gram = lax.psum(share, ('wide', 'narrow'))  76.5 us
    dot_general x64, matrix products, lower_inverse(): jnp.dot(lower[line, :], result, precision=lax.Precision.HIGHEST, preferre...  49 us
    slice x63, local copies, waits for them, and re-layouts, cholesky_lower(): pivot = jnp.sqrt(partial_col[column])  37.6 us
  transfers between devices with their start and end apart: 5, of which 4 were waited for; matrix products, arithmetic and copies ran while one was open for 13% of the time, Pallas kernels for 0%

commit v1 on v0

v1 whole, which is shorter than its diff:
```python
import functools
import math

import jax
import jax.numpy as jnp
import numpy as np
from jax import lax
from jax.experimental import pallas as pl
from jax.experimental.pallas import tpu as pltpu
from jax.sharding import PartitionSpec as P

MESH = pl.DeviceIdType.MESH
F32 = jnp.float32
BF16 = jnp.bfloat16
NT = (((1,), (1,)), ((), ()))

N_Y, N_X, N_CORE, N_Z = 4, 4, 2, 8
PLANE = N_Y * N_X
COLS = 64
COUNT = 16384
GROUP = 8
CHUNKS = COLS // GROUP
HALF = CHUNKS // 2
Z_LEN = COUNT // N_Z
P_LEN = COUNT // PLANE
INNER = 256


def sylvester(order):
    matrix = np.ones((1, 1), np.float32)
    while matrix.shape[0] < order:
        matrix = np.block([[matrix, matrix], [matrix, -matrix]])
    return matrix


def butterflies(parts):
    parts = list(parts)
    half = 1
    while half < len(parts):
        for low in range(len(parts)):
            if not low & half:
                first, second = parts[low], parts[low | half]
                parts[low], parts[low | half] = first + second, first - second
        half *= 2
    return parts


def lanes(start, size):
    return pl.ds(pl.multiple_of(start, 128), size)


def device(y, x, core, z):
    return (((y % N_Y) * N_X + x % N_X) * N_CORE + core % N_CORE, z % N_Z)


def mix_kernel(
    panel_ref, signs_ref, samples_ref, h_ref, mixed_ref, gram_ref,
    panel, s0, r1, s1, r2, s2, r3, s3, r4, e, tw, weight, g_own, g_z, g_zsum, g_plane,
    in_sem, out_sem, send1, recv1, send2, recv2, send3, recv3, send4, recv4,
    send_core, recv_core, send_gz, recv_gz, send_gp, recv_gp, send_gg, recv_gg,
):
    wide = lax.axis_index("wide")
    z = lax.axis_index("narrow")
    core = wide % N_CORE
    x = (wide // N_CORE) % N_X
    y = wide // (N_CORE * N_X)
    q = wide // N_CORE
    z_peers = [device(y, x, core, z + d) for d in range(1, N_Z)]
    z_index = [(z + d) % N_Z for d in range(1, N_Z)]
    xy_offsets = [(a, b) for a in range(N_Y) for b in range(N_X) if a or b]
    xy_peers = [device(y + a, x + b, core, z) for a, b in xy_offsets]
    xy_index = [((y + a) % N_Y) * N_X + (x + b) % N_X for a, b in xy_offsets]
    sibling = device(y, x, core + 1, z)
    crossed = [device(y + a, x + b, core + 1, z) for a, b in xy_offsets]
    plane_peers = xy_peers + [sibling] + crossed

    def load(c):
        return pltpu.make_async_copy(
            panel_ref.at[pl.ds(pl.multiple_of(c * GROUP, GROUP), GROUP)], panel.at[c], in_sem.at[c]
        )

    for i in range(HALF):
        load(i).start()
        load(HALF + i).start()

    barrier = pltpu.get_barrier_semaphore()
    for peer in z_peers + plane_peers:
        pl.semaphore_signal(barrier, inc=1, device_id=peer, device_id_type=MESH)
    pl.semaphore_wait(barrier, len(z_peers) + len(plane_peers))

    def send(over_z, src, dst, c, send_sem, recv_sem):
        size = Z_LEN if over_z else P_LEN
        mine = (z if over_z else q) * size
        peers, index = (z_peers, z_index) if over_z else (xy_peers, xy_index)
        for peer, place in zip(peers, index):
            pltpu.make_async_remote_copy(
                src_ref=src.at[c, :, lanes(place * size, size)],
                dst_ref=dst.at[c, :, lanes(mine, size)],
                send_sem=send_sem.at[c],
                recv_sem=recv_sem.at[c],
                device_id=peer,
                device_id_type=MESH,
            ).start()

    def await_bytes(over_z, ref, c, sem):
        part = ref.at[c, :, pl.ds(0, COUNT - (Z_LEN if over_z else P_LEN))]
        pltpu.make_async_copy(part, part, sem.at[c]).wait()

    def combine(over_z, own, got, out, back, c):
        size = Z_LEN if over_z else P_LEN
        n = N_Z if over_z else PLANE
        mine = lanes((z if over_z else q) * size, size)
        got[c, :, mine] = own[c, :, mine]
        step = 4096 // n

        def part(i, carry):
            places = [lanes(p * size + i * step, step) for p in range(n)]
            values = butterflies([got[c, :, place] for place in places])
            for place, value in zip(places, values):
                out[c, :, place] = value
            return carry

        lax.fori_loop(0, size // step, part, 0)
        back[c, :, mine] = out[c, :, mine]

    def core_copy(c):
        return pltpu.make_async_remote_copy(
            src_ref=r2.at[c], dst_ref=e.at[c], send_sem=send_core.at[c], recv_sem=recv_core.at[c],
            device_id=sibling, device_id_type=MESH,
        )

    flip = 1.0 - 2.0 * core.astype(F32)

    def core_combine(c):
        core_copy(c).start()
        core_copy(c).wait_recv()

        def part(i, carry):
            place = lanes(i * 2048, 2048)
            s2[c, :, place] = e[c, :, place] + flip * r2[c, :, place]
            return carry

        lax.fori_loop(0, COUNT // 2048, part, 0)

    def mix(c):
        load(c).wait()

        def slab(i, carry):
            place = lanes(i * 1024, 1024)
            values = panel[c, :, place] * signs_ref[:, place].astype(F32)
            low = values - values.astype(BF16).astype(F32)
            rows = []
            for b in range(1024 // INNER):
                rows += [values[:, b * INNER:(b + 1) * INNER], low[:, b * INNER:(b + 1) * INNER]]
            stacked = jnp.concatenate(rows, axis=0).astype(BF16)
            done = jnp.dot(stacked, h_ref[...], preferred_element_type=F32)
            parts = [
                done[16 * b:16 * b + 8] + done[16 * b + 8:16 * b + 16] for b in range(1024 // INNER)
            ]
            s0[c, :, place] = jnp.concatenate(butterflies(parts), axis=1)
            return carry

        lax.fori_loop(0, COUNT // 1024, slab, 0)

        def part(i, carry):
            places = [lanes(p * 1024 + i * 256, 256) for p in range(16)]
            values = butterflies([s0[c, :, place] for place in places])
            for place, value in zip(places, values):
                s0[c, :, place] = value
            return carry

        lax.fori_loop(0, 4, part, 0)

    def begin(i, carry):
        mix(i)
        send(True, s0, r1, i, send1, recv1)
        mix(HALF + i)
        send(False, s0, r1, HALF + i, send1, recv1)
        return carry

    lax.fori_loop(0, HALF, begin, 0)

    base = (wide * N_Z + z) * COUNT
    weight[...] = jnp.zeros_like(weight)

    def mark(i, carry):
        offsets = samples_ref[pl.ds(i * 8, 8), :] - base
        high = jnp.right_shift(offsets, 7)
        low = jnp.bitwise_and(offsets, 127)
        places = lax.broadcasted_iota(jnp.int32, (128, 128), 0)
        total = jnp.zeros((128, 128), F32)
        for r in range(0, 8, 2):
            above = [jnp.where(places == high[k:k + 1], 1.0, 0.0) for k in (r, r + 1)]
            below = [jnp.where(places == low[k:k + 1], 1.0, 0.0) for k in (r, r + 1)]
            total += lax.dot_general(
                jnp.concatenate(above, axis=1).astype(BF16),
                jnp.concatenate(below, axis=1).astype(BF16),
                NT,
                preferred_element_type=F32,
            )
        weight[...] += total
        return carry

    lax.fori_loop(0, 16, mark, 0)

    def second(i, carry):
        b = HALF + i
        await_bytes(False, r1, b, recv1)
        combine(False, s0, r1, s1, r2, b)
        send(False, s1, r2, b, send2, recv2)
        await_bytes(True, r1, i, recv1)
        combine(True, s0, r1, s1, r2, i)
        send(True, s1, r2, i, send2, recv2)
        return carry

    lax.fori_loop(0, HALF, second, 0)

    def third(i, carry):
        b = HALF + i
        await_bytes(False, r2, b, recv2)
        core_combine(b)
        send(True, s2, r3, b, send3, recv3)
        return carry

    lax.fori_loop(0, HALF, third, 0)

    def fourth(i, carry):
        await_bytes(True, r2, i, recv2)
        core_combine(i)
        send(False, s2, r3, i, send3, recv3)
        return carry

    lax.fori_loop(0, HALF, fourth, 0)

    def fifth(i, carry):
        await_bytes(False, r3, i, recv3)
        combine(False, s2, r3, s3, r4, i)
        send(False, s3, r4, i, send4, recv4)
        return carry

    lax.fori_loop(0, HALF, fifth, 0)

    def store(c):
        return pltpu.make_async_copy(
            r4.at[c], mixed_ref.at[pl.ds(pl.multiple_of(c * GROUP, GROUP), GROUP)], out_sem.at[c]
        )

    def final(c):
        store(c).start()

        def slab(i, carry):
            place = lanes(i * 1024, 1024)
            rows = weight[pl.ds(pl.multiple_of(i * 8, 8), 8), :]
            mask = jnp.concatenate([rows[k:k + 1] for k in range(8)], axis=1)
            values = r4[c, :, place] * mask
            low = values - values.astype(BF16).astype(F32)
            both = jnp.concatenate([values, low], axis=0).astype(BF16)
            tw[pl.ds(pl.multiple_of(c * 16, 16), 16), place] = both
            return carry

        lax.fori_loop(0, COUNT // 1024, slab, 0)

    def sixth(i, carry):
        b = HALF + i
        await_bytes(True, r3, b, recv3)
        combine(True, s2, r3, s3, r4, b)
        send(True, s3, r4, b, send4, recv4)
        await_bytes(False, r4, i, recv4)
        final(i)
        return carry

    lax.fori_loop(0, HALF, sixth, 0)

    def seventh(i, carry):
        b = HALF + i
        await_bytes(True, r4, b, recv4)
        final(b)
        return carry

    lax.fori_loop(0, HALF, seventh, 0)

    def product(i, total):
        part = tw[:, lanes(i * 2048, 2048)]
        return total + lax.dot_general(part, part, NT, preferred_element_type=F32)

    total = lax.fori_loop(0, COUNT // 2048, product, jnp.zeros((128, 128), F32))
    rows = jnp.concatenate(
        [total[16 * c:16 * c + 8] + total[16 * c + 8:16 * c + 16] for c in range(CHUNKS)], axis=0
    )
    lane = lax.broadcasted_iota(jnp.int32, (128, 128), 0)
    column = lax.broadcasted_iota(jnp.int32, (128, 128), 1)
    chosen = jnp.where((lane // 16) * 8 + lane % 8 == column, 1.0, 0.0)
    g_own[...] = jnp.dot(rows, chosen, precision=lax.Precision.HIGHEST, preferred_element_type=F32)

    def rows_of(place):
        return pl.ds(pl.multiple_of(place * GROUP, GROUP), GROUP)

    for peer, place in zip(z_peers, z_index):
        pltpu.make_async_remote_copy(
            src_ref=g_own.at[rows_of(place)], dst_ref=g_z.at[z], send_sem=send_gz.at[0],
            recv_sem=recv_gz.at[0], device_id=peer, device_id_type=MESH,
        ).start()
    g_z[z] = g_own[rows_of(z)]
    others = g_z.at[pl.ds(0, N_Z - 1)]
    pltpu.make_async_copy(others, others, recv_gz.at[0]).wait()
    g_zsum[...] = functools.reduce(lambda a, b: a + b, [g_z[k] for k in range(N_Z)])
    for peer in plane_peers:
        pltpu.make_async_remote_copy(
            src_ref=g_zsum, dst_ref=g_plane.at[wide], send_sem=send_gp.at[0],
            recv_sem=recv_gp.at[0], device_id=peer, device_id_type=MESH,
        ).start()
    g_plane[wide] = g_zsum[...]
    planes = g_plane.at[pl.ds(0, PLANE * N_CORE - 1)]
    pltpu.make_async_copy(planes, planes, recv_gp.at[0]).wait()
    gram_ref[rows_of(z)] = functools.reduce(
        lambda a, b: a + b, [g_plane[k] for k in range(PLANE * N_CORE)]
    )
    for peer in z_peers:
        pltpu.make_async_remote_copy(
            src_ref=gram_ref.at[rows_of(z)], dst_ref=gram_ref.at[rows_of(z)], send_sem=send_gg.at[0],
            recv_sem=recv_gg.at[0], device_id=peer, device_id_type=MESH,
        ).start()
    bands = gram_ref.at[pl.ds(0, COLS - GROUP)]
    pltpu.make_async_copy(bands, bands, recv_gg.at[0]).wait()

    pltpu.make_async_copy(others, others, send_gz.at[0]).wait()
    pltpu.make_async_copy(planes, planes, send_gp.at[0]).wait()
    pltpu.make_async_copy(bands, bands, send_gg.at[0]).wait()

    def drain(i, carry):
        b = HALF + i
        await_bytes(True, s0, i, send1)
        await_bytes(False, s0, b, send1)
        await_bytes(True, s1, i, send2)
        await_bytes(False, s1, b, send2)
        await_bytes(False, s2, i, send3)
        await_bytes(True, s2, b, send3)
        await_bytes(False, s3, i, send4)
        await_bytes(True, s3, b, send4)
        core_copy(i).wait_send()
        core_copy(b).wait_send()
        store(i).wait()
        store(b).wait()
        return carry

    lax.fori_loop(0, HALF, drain, 0)


def finish_kernel(
    scale, root, gram_ref, panel_ref, mixed_in, mixed_ref, r_ref, precond_ref,
    panel, out, mixed_sem, in_sem, out_sem,
):
    copy_mixed = pltpu.make_async_copy(mixed_in, mixed_ref, mixed_sem)
    copy_mixed.start()
    copy_panel = pltpu.make_async_copy(panel_ref, panel, in_sem)
    copy_panel.start()
    row = lax.broadcasted_iota(jnp.int32, (COLS, 2 * COLS), 0)
    column = lax.broadcasted_iota(jnp.int32, (COLS, 2 * COLS), 1)
    start = jnp.where(
        column < COLS, gram_ref[...] * scale, jnp.where(column - COLS == row, 1.0, 0.0)
    )
    bands = [start[8 * b:8 * b + 8] for b in range(COLS // 8)]
    sub = lax.broadcasted_iota(jnp.int32, (8, 1), 0)
    roots = []
    for k in range(COLS):
        home = k // 8
        line = bands[home][k % 8:k % 8 + 1]
        pivot = line[:, k:k + 1]
        roots.append(pivot)
        scaled = line / pivot
        for b in range(home, COLS // 8):
            factor = bands[b][:, k:k + 1]
            if b == home:
                factor = jnp.where(sub > k % 8, factor, 0.0)
            bands[b] = bands[b] - factor * scaled
    done = jnp.concatenate(bands, axis=0)
    diagonal = jnp.sqrt(jnp.concatenate(roots, axis=0))
    done = done / diagonal
    square = done[:, :COLS]
    upper = lax.broadcasted_iota(jnp.int32, (COLS, COLS), 1) >= lax.broadcasted_iota(
        jnp.int32, (COLS, COLS), 0
    )
    r_ref[...] = jnp.where(upper, square * (1.0 / root), 0.0)
    inverse = done[:, COLS:] * root
    high = inverse.astype(BF16)
    low = (inverse - high.astype(F32)).astype(BF16)
    left = jnp.concatenate([high, low, high], axis=1)

    copy_panel.wait()

    def tile(i):
        place = lanes(i * 1024, 1024)
        return pltpu.make_async_copy(out.at[:, place], precond_ref.at[:, place], out_sem.at[i])

    def multiply(i, carry):
        place = lanes(i * 1024, 1024)
        values = panel[:, place]
        values_high = values.astype(BF16)
        values_low = (values - values_high.astype(F32)).astype(BF16)
        right = jnp.concatenate([values_high, values_high, values_low], axis=0)
        out[:, place] = jnp.dot(left, right, preferred_element_type=F32)
        tile(i).start()
        return carry

    lax.fori_loop(0, COUNT // 1024, multiply, 0)

    def drain(i, carry):
        tile(i).wait()
        return carry

    lax.fori_loop(0, COUNT // 1024, drain, 0)
    copy_mixed.wait()


def body(panel, signs, sample_rows):
    cols, count = panel.shape
    total = count * lax.axis_size("wide") * lax.axis_size("narrow")
    root = math.sqrt(total)
    any_space = pl.BlockSpec(memory_space=pl.ANY)
    vmem = pl.BlockSpec(memory_space=pltpu.VMEM)
    mixer = jnp.asarray(sylvester(INNER) / root, BF16)
    chunked = pltpu.VMEM((CHUNKS, GROUP, count), F32)
    dma = pltpu.SemaphoreType.DMA
    mixed, gram = pl.pallas_call(
        mix_kernel,
        out_shape=(
            jax.ShapeDtypeStruct((cols, count), F32),
            jax.ShapeDtypeStruct((cols, 128), F32),
        ),
        in_specs=[any_space, vmem, vmem, vmem],
        out_specs=(any_space, vmem),
        scratch_shapes=[chunked] * 10
        + [
            pltpu.VMEM((2 * cols, count), BF16),
            pltpu.VMEM((128, 128), F32),
            pltpu.VMEM((cols, 128), F32),
            pltpu.VMEM((N_Z, GROUP, 128), F32),
            pltpu.VMEM((GROUP, 128), F32),
            pltpu.VMEM((PLANE * N_CORE, GROUP, 128), F32),
        ]
        + [dma((CHUNKS,))] * 12
        + [dma((1,))] * 6,
        compiler_params=pltpu.CompilerParams(
            collective_id=0, has_side_effects=True, vmem_limit_bytes=56 * 1024 * 1024
        ),
    )(panel, signs.reshape(1, count), sample_rows.reshape(-1, 128), mixer)
    mixed, r_factor, precond = pl.pallas_call(
        functools.partial(finish_kernel, total / sample_rows.shape[0], root),
        out_shape=(
            jax.ShapeDtypeStruct((cols, count), F32),
            jax.ShapeDtypeStruct((cols, cols), F32),
            jax.ShapeDtypeStruct((cols, count), F32),
        ),
        in_specs=[vmem, any_space, any_space],
        out_specs=(any_space, vmem, any_space),
        scratch_shapes=[
            pltpu.VMEM((cols, count), F32),
            pltpu.VMEM((cols, count), F32),
            dma,
            dma,
            dma((count // 1024,)),
        ],
        compiler_params=pltpu.CompilerParams(vmem_limit_bytes=40 * 1024 * 1024),
    )(gram, panel, mixed)
    return (mixed, r_factor, precond)


def solution(mesh):
    in_specs = (P(None, ("wide", "narrow")), P(("wide", "narrow")), P())
    out_specs = (P(None, ("wide", "narrow")), P(), P(None, ("wide", "narrow")))
    return jax.shard_map(body, mesh=mesh, in_specs=in_specs, out_specs=out_specs, check_vma=False)
```

time: 984 us -> 229 us (0.23)
  waiting for transfers between devices: 277 us -> 0 us
  blocking collectives: 276 us -> 0 us
  Pallas kernels: 0 us -> 225 us
  other arithmetic: 200 us -> 0 us
  matrix products: 87.1 us -> 0 us
  local copies, waits for them, and re-layouts: 78 us -> 2.94 us
  between operations: 45.7 us -> 0.66 us
  starting transfers between devices: 12.3 us -> 0 us
    ppermute x5 -> x0, waiting for transfers between devices: 277 us -> none  [swapped(): return lax.ppermute(block, axis, route)]
    pallas_call x0 -> x2, Pallas kernels: none -> 225 us  [the longest x1 215 us: body(): pl.pallas_call(mix_kernel, out_shape=(jax.ShapeDtypeStruct((cols, count),...]
    all_to_all x2 -> x0, blocking collectives: 199 us -> none  [the longest x1 104 us: body(): lax.all_to_all(shaped, 'narrow', split_axis=1, concat_axis=1, tiled=True)]
    dot_general x133 -> x0, matrix products: 87.1 us -> none  [the longest x64 49 us: lower_inverse(): jnp.dot(lower[line, :], result, precision=lax.Precision.HIGHEST, preferre...]
    scatter-add x1 -> x0, other arithmetic: 85.8 us -> none  [body(): weight = jnp.zeros((count,), jnp.float32).at[offsets].add(1.0, mode='drop')]
    another operation x127 -> x0, other arithmetic: 82 us -> none
    psum x1 -> x0, blocking collectives: 76.5 us -> none  [body(): gram = lax.psum(share, ('wide', 'narrow'))]
    slice x139 -> x0, local copies, waits for them, and re-layouts: 56.4 us -> none  [the longest x63 37.6 us: cholesky_lower(): pivot = jnp.sqrt(partial_col[column])]
  transfers between devices with their start and end apart: 5 -> 0, of which waited for: 4 -> 0; matrix products, arithmetic and copies ran while one was open for 13% -> 0% of each run, Pallas kernels for 0% -> 0%
where the time goes in v1:
time: 229 us
  Pallas kernels  225 us (98%)
  local copies, waits for them, and re-layouts  2.94 us (1%)
    pallas_call x1, Pallas kernels, body(): pl.pallas_call(mix_kernel, out_shape=(jax.ShapeDtypeStruct((cols, count),...  215 us
    pallas_call x1, Pallas kernels, body(): pl.pallas_call(functools.partial(finish_kernel, total / sample_rows.shape...  10.3 us

profile of v1, /device:TPU:1, one launch (start us, length us, event | category | flops | bytes accessed | tf_op | source)
XLA Modules:
  0.0 228.8 jit_solution(17697851582102064982)
XLA Ops:
  0.6 0.0 copy-start
  0.6 214.9 %shard_map.67 = (f32[64,16384]{1,0:T(8,128)}, f32[64,128]{1,0:T(8,128)}) custom-call(f32[64,16384]{1,0:T(8,128)} %panel_ref.3, s32[1,16384]{1,0:T(1,128)} %bitcast.2, s32[128,128]{1,0:T(8,128)} %bitcast.3, bf16[256,256]{1,0:T(8,128)(2,1)} %constant.2.clone.h_ref), custom_call_target="tpu_custom_call" | custom-call | tf_op jit(solution)/shard_map/pallas_call | solution.py:424
  215.6 0.0 copy-done
  215.6 0.0 copy-start.1
  215.6 2.2 copy-done.1
  217.8 0.0 copy-start.2
  217.8 0.8 copy-done.2
  218.5 10.3 %shard_map.68 = (f32[64,16384]{1,0:T(8,128)}, f32[64,64]{1,0:T(8,128)}, f32[64,16384]{1,0:T(8,128)}) custom-call(f32[64,128]{1,0:T(8,128)S(1)} %copy-done.2, f32[64,16384]{1,0:T(8,128)S(1)} %copy-done, f32[64,16384]{1,0:T(8,128)S(1)} %copy-done.1), custom_call_target="tpu_custom_call" | custom-call | tf_op jit(solution)/shard_map/pallas_call | solution.py:447
Async XLA Ops:
  0.6 215.0 %copy-start = (f32[64,16384]{1,0:T(8,128)S(1)}, f32[64,16384]{1,0:T(8,128)}, u32[]{:S(2)}) copy-start(f32[64,16384]{1,0:T(8,128)} %panel_ref.3) | copy-start | bytes 12582916
  215.6 2.2 copy-start.1
  217.8 0.8 copy-start.2

commit v2 on v1

v2 whole, which is shorter than its diff:
```python
import functools
import math

import jax
import jax.numpy as jnp
import numpy as np
from jax import lax
from jax.experimental import pallas as pl
from jax.experimental.pallas import tpu as pltpu
from jax.sharding import PartitionSpec as P

MESH = pl.DeviceIdType.MESH
F32 = jnp.float32
BF16 = jnp.bfloat16
NT = (((1,), (1,)), ((), ()))

N_Y, N_X, N_CORE, N_Z = 4, 4, 2, 8
PLANE = N_Y * N_X
COLS = 64
COUNT = 16384
GROUP = 8
CHUNKS = COLS // GROUP
AHEAD = 4
Z_LEN = COUNT // N_Z
P_LEN = COUNT // PLANE
INNER = 256


def sylvester(order):
    matrix = np.ones((1, 1), np.float32)
    while matrix.shape[0] < order:
        matrix = np.block([[matrix, matrix], [matrix, -matrix]])
    return matrix


def butterflies(parts):
    parts = list(parts)
    half = 1
    while half < len(parts):
        for low in range(len(parts)):
            if not low & half:
                first, second = parts[low], parts[low | half]
                parts[low], parts[low | half] = first + second, first - second
        half *= 2
    return parts


def lanes(start, size):
    return pl.ds(pl.multiple_of(start, 128), size)


def device(y, x, core, z):
    return (((y % N_Y) * N_X + x % N_X) * N_CORE + core % N_CORE, z % N_Z)


def mix_kernel(
    scale, root, panel_ref, signs_ref, samples_ref, h_ref, mixed_ref, r_ref, precond_ref,
    panel, s0, r1, s1, r2, s2, r3, e, s3, out, tw, weight, g_own, g_z, g_zsum, g_plane, gram,
    in_sem, own_sem, out_sem, send1, recv1, send2, recv2, send3, recv3, send4, recv4,
    send_core, recv_core, send_gz, recv_gz, send_gp, recv_gp, send_gg, recv_gg,
):
    wide = lax.axis_index("wide")
    z = lax.axis_index("narrow")
    core = wide % N_CORE
    x = (wide // N_CORE) % N_X
    y = wide // (N_CORE * N_X)
    q = wide // N_CORE
    z_peers = [device(y, x, core, z + d) for d in range(1, N_Z)]
    z_index = [(z + d) % N_Z for d in range(1, N_Z)]
    xy_offsets = [(a, b) for a in range(N_Y) for b in range(N_X) if a or b]
    xy_peers = [device(y + a, x + b, core, z) for a, b in xy_offsets]
    xy_index = [((y + a) % N_Y) * N_X + (x + b) % N_X for a, b in xy_offsets]
    sibling = device(y, x, core + 1, z)
    crossed = [device(y + a, x + b, core + 1, z) for a, b in xy_offsets]
    plane_peers = xy_peers + [sibling] + crossed

    def band(c):
        return pl.ds(pl.multiple_of(c * GROUP, GROUP), GROUP)

    def load(c):
        return pltpu.make_async_copy(panel_ref.at[band(c)], panel.at[c], in_sem.at[c])

    for c in range(CHUNKS):
        load(c).start()

    barrier = pltpu.get_barrier_semaphore()
    for peer in z_peers + plane_peers:
        pl.semaphore_signal(barrier, inc=1, device_id=peer, device_id_type=MESH)

    def send(over_z, src, target, c, send_sem, recv_sem):
        size = Z_LEN if over_z else P_LEN
        peers, index = (z_peers, z_index) if over_z else (xy_peers, xy_index)
        for peer, place in zip(peers, index):
            pltpu.make_async_remote_copy(
                src_ref=src.at[c, :, lanes(place * size, size)],
                dst_ref=target(lanes((z if over_z else q) * size, size)),
                send_sem=send_sem.at[c],
                recv_sem=recv_sem.at[c],
                device_id=peer,
                device_id_type=MESH,
            ).start()

    def await_bytes(over_z, ref, c, sem):
        part = ref.at[c, :, pl.ds(0, COUNT - (Z_LEN if over_z else P_LEN))]
        pltpu.make_async_copy(part, part, sem.at[c]).wait()

    def combine(over_z, own, got, out, c):
        size = Z_LEN if over_z else P_LEN
        n = N_Z if over_z else PLANE
        mine = lanes((z if over_z else q) * size, size)
        got[c, :, mine] = own[c, :, mine]
        step = 4096 // n

        def part(i, carry):
            places = [lanes(p * size + i * step, step) for p in range(n)]
            values = butterflies([got[c, :, place] for place in places])
            for place, value in zip(places, values):
                out[c, :, place] = value
            return carry

        lax.fori_loop(0, size // step, part, 0)

    def mix(c):
        load(c).wait()

        def slab(i, carry):
            place = lanes(i * 1024, 1024)
            values = panel[c, :, place] * signs_ref[:, place].astype(F32)
            low = values - values.astype(BF16).astype(F32)
            rows = []
            for b in range(1024 // INNER):
                rows += [values[:, b * INNER:(b + 1) * INNER], low[:, b * INNER:(b + 1) * INNER]]
            stacked = jnp.concatenate(rows, axis=0).astype(BF16)
            done = jnp.dot(stacked, h_ref[...], preferred_element_type=F32)
            parts = [
                done[16 * b:16 * b + 8] + done[16 * b + 8:16 * b + 16] for b in range(1024 // INNER)
            ]
            s0[c, :, place] = jnp.concatenate(butterflies(parts), axis=1)
            return carry

        lax.fori_loop(0, COUNT // 1024, slab, 0)

        def part(i, carry):
            places = [lanes(p * 1024 + i * 256, 256) for p in range(16)]
            values = butterflies([s0[c, :, place] for place in places])
            for place, value in zip(places, values):
                s0[c, :, place] = value
            return carry

        lax.fori_loop(0, 4, part, 0)

    def send_z(c):
        send(True, s0, lambda place: r1.at[c, :, place], c, send1, recv1)

    mix(0)
    pl.semaphore_wait(barrier, len(z_peers) + len(plane_peers))
    send_z(0)

    def begin(c, carry):
        mix(c)
        send_z(c)
        return carry

    lax.fori_loop(1, CHUNKS, begin, 0)

    weight[...] = jnp.zeros_like(weight)

    def mark(i, carry):
        rows = samples_ref[pl.ds(pl.multiple_of(i * 8, 8), 8), :]
        offsets = rows - wide * (N_Z * COUNT)
        place = jnp.bitwise_and(jnp.right_shift(offsets, 11), N_Z - 1)
        inside = (jnp.right_shift(offsets, 17) == 0) & (place == z)
        inner = jnp.bitwise_and(jnp.right_shift(offsets, 7), Z_LEN // 128 - 1)
        high = jnp.where(inside, jnp.right_shift(offsets, 14) * (Z_LEN // 128) + inner, -1)
        low = jnp.bitwise_and(offsets, 127)
        places = lax.broadcasted_iota(jnp.int32, (128, 128), 0)
        total = jnp.zeros((128, 128), F32)
        for r in range(0, 8, 2):
            above = [jnp.where(places == high[k:k + 1], 1.0, 0.0) for k in (r, r + 1)]
            below = [jnp.where(places == low[k:k + 1], 1.0, 0.0) for k in (r, r + 1)]
            total += lax.dot_general(
                jnp.concatenate(above, axis=1).astype(BF16),
                jnp.concatenate(below, axis=1).astype(BF16),
                NT,
                preferred_element_type=F32,
            )
        weight[...] += total
        return carry

    lax.fori_loop(0, 16, mark, 0)

    def plane_out(c):
        await_bytes(True, r1, c, recv1)
        combine(True, s0, r1, s1, c)
        send(False, s1, lambda place: r2.at[c, :, place], c, send2, recv2)

    def plane_back(c):
        await_bytes(False, r2, c, recv2)
        combine(False, s1, r2, s2, c)
        send(False, s2, lambda place: r3.at[c, :, place], c, send3, recv3)

    def core_copy(c):
        return pltpu.make_async_remote_copy(
            src_ref=r3.at[c], dst_ref=e.at[c], send_sem=send_core.at[c], recv_sem=recv_core.at[c],
            device_id=sibling, device_id_type=MESH,
        )

    def core_out(c):
        await_bytes(False, r3, c, recv3)
        mine = lanes(q * P_LEN, P_LEN)
        r3[c, :, mine] = s2[c, :, mine]
        core_copy(c).start()

    flip = 1.0 - 2.0 * core.astype(F32)

    def keep(c):
        mine = lanes(z * Z_LEN, Z_LEN)
        return pltpu.make_async_copy(s3.at[c, :, mine], mixed_ref.at[band(c), mine], own_sem.at[c])

    def last(c):
        core_copy(c).wait_recv()

        def slab(i, carry):
            place = lanes(i * 1024, 1024)
            values = e[c, :, place] + flip * r3[c, :, place]
            s3[c, :, place] = values
            rows = weight[pl.ds(pl.multiple_of(i * 8, 8), 8), :]
            mask = jnp.concatenate([rows[k:k + 1] for k in range(8)], axis=1)
            values = values * mask
            low = values - values.astype(BF16).astype(F32)
            both = jnp.concatenate([values, low], axis=0).astype(BF16)
            tw[pl.ds(pl.multiple_of(c * 16, 16), 16), place] = both
            return carry

        lax.fori_loop(0, COUNT // 1024, slab, 0)
        keep(c).start()

    def z_back(c, carry):
        send(True, s3, lambda place: mixed_ref.at[band(c), place], c, send4, recv4)
        return carry

    def step(c, carry):
        plane_out(c)
        plane_back(c - 1)
        core_out(c - 2)
        last(c - 2)
        return carry

    def early(c, carry):
        step(c, carry)
        z_back(c - 2, carry)
        return carry

    plane_out(0)
    plane_out(1)
    plane_back(0)
    lax.fori_loop(2, AHEAD + 2, early, 0)
    lax.fori_loop(AHEAD + 2, CHUNKS, step, 0)
    plane_back(CHUNKS - 1)
    core_out(CHUNKS - 2)
    last(CHUNKS - 2)
    core_out(CHUNKS - 1)
    last(CHUNKS - 1)

    def product(i, total):
        part = tw[:, lanes(i * 2048, 2048)]
        return total + lax.dot_general(part, part, NT, preferred_element_type=F32)

    total = lax.fori_loop(0, COUNT // 2048, product, jnp.zeros((128, 128), F32))
    rows = jnp.concatenate(
        [total[16 * c:16 * c + 8] + total[16 * c + 8:16 * c + 16] for c in range(CHUNKS)], axis=0
    )
    lane = lax.broadcasted_iota(jnp.int32, (128, 128), 0)
    column = lax.broadcasted_iota(jnp.int32, (128, 128), 1)
    chosen = jnp.where((lane // 16) * 8 + lane % 8 == column, 1.0, 0.0)
    g_own[...] = jnp.dot(rows, chosen, precision=lax.Precision.HIGHEST, preferred_element_type=F32)

    for peer, place in zip(z_peers, z_index):
        pltpu.make_async_remote_copy(
            src_ref=g_own.at[band(place)], dst_ref=g_z.at[z], send_sem=send_gz.at[0],
            recv_sem=recv_gz.at[0], device_id=peer, device_id_type=MESH,
        ).start()
    z_back(AHEAD, 0)
    g_z[z] = g_own[band(z)]
    others = g_z.at[pl.ds(0, N_Z - 1)]
    pltpu.make_async_copy(others, others, recv_gz.at[0]).wait()
    g_zsum[...] = functools.reduce(lambda a, b: a + b, [g_z[k] for k in range(N_Z)])
    for peer in plane_peers:
        pltpu.make_async_remote_copy(
            src_ref=g_zsum, dst_ref=g_plane.at[wide], send_sem=send_gp.at[0],
            recv_sem=recv_gp.at[0], device_id=peer, device_id_type=MESH,
        ).start()
    g_plane[wide] = g_zsum[...]
    planes = g_plane.at[pl.ds(0, PLANE * N_CORE - 1)]
    pltpu.make_async_copy(planes, planes, recv_gp.at[0]).wait()
    gram[band(z)] = functools.reduce(
        lambda a, b: a + b, [g_plane[k] for k in range(PLANE * N_CORE)]
    )
    for peer in z_peers:
        pltpu.make_async_remote_copy(
            src_ref=gram.at[band(z)], dst_ref=gram.at[band(z)], send_sem=send_gg.at[0],
            recv_sem=recv_gg.at[0], device_id=peer, device_id_type=MESH,
        ).start()
    lax.fori_loop(AHEAD + 1, CHUNKS, z_back, 0)
    bands = gram.at[pl.ds(0, COLS - GROUP)]
    pltpu.make_async_copy(bands, bands, recv_gg.at[0]).wait()

    row = lax.broadcasted_iota(jnp.int32, (COLS, 2 * COLS), 0)
    column = lax.broadcasted_iota(jnp.int32, (COLS, 2 * COLS), 1)
    start = jnp.where(
        column < COLS, gram[...] * scale, jnp.where(column - COLS == row, 1.0, 0.0)
    )

    def eliminate(k, values):
        line = jnp.sum(jnp.where(row == k, values, 0.0), axis=0, keepdims=True)
        factor = jnp.sum(jnp.where((column == k) & (row > k), values, 0.0), axis=1, keepdims=True)
        pivot = jnp.sum(jnp.where(column[:1] == k, line, 0.0), axis=1, keepdims=True)
        return values - factor * (line / pivot)

    done = lax.fori_loop(0, COLS, eliminate, start)
    diagonal = jnp.sum(jnp.where(row == column, done, 0.0), axis=1, keepdims=True)
    done = done / jnp.sqrt(diagonal)
    square = done[:, :COLS]
    r_ref[...] = jnp.where(row[:, :COLS] <= column[:, :COLS], square * (1.0 / root), 0.0)
    inverse = done[:, COLS:] * root
    high = inverse.astype(BF16)
    low = (inverse - high.astype(F32)).astype(BF16)
    left = jnp.concatenate([high, low, high], axis=1)

    def tile(i):
        place = lanes(i * 1024, 1024)
        return pltpu.make_async_copy(out.at[:, place], precond_ref.at[:, place], out_sem.at[i])

    def multiply(i, carry):
        place = lanes(i * 1024, 1024)
        values = jnp.concatenate([panel[c, :, place] for c in range(CHUNKS)], axis=0)
        values_high = values.astype(BF16)
        values_low = (values - values_high.astype(F32)).astype(BF16)
        right = jnp.concatenate([values_high, values_high, values_low], axis=0)
        out[:, place] = jnp.dot(left, right, preferred_element_type=F32)
        tile(i).start()
        return carry

    lax.fori_loop(0, COUNT // 1024, multiply, 0)

    pltpu.make_async_copy(others, others, send_gz.at[0]).wait()
    pltpu.make_async_copy(planes, planes, send_gp.at[0]).wait()
    pltpu.make_async_copy(bands, bands, send_gg.at[0]).wait()

    def drain(i, carry):
        tile(i).wait()
        return carry

    lax.fori_loop(0, COUNT // 1024, drain, 0)

    def arrived(c, carry):
        await_bytes(True, s0, c, send1)
        await_bytes(False, s1, c, send2)
        await_bytes(False, s2, c, send3)
        core_copy(c).wait_send()
        keep(c).wait()
        await_bytes(True, s3, c, send4)
        part = mixed_ref.at[band(c), pl.ds(0, COUNT - Z_LEN)]
        pltpu.make_async_copy(part, part, recv4.at[c]).wait()
        return carry

    lax.fori_loop(0, CHUNKS, arrived, 0)


def body(panel, signs, sample_rows):
    cols, count = panel.shape
    total = count * lax.axis_size("wide") * lax.axis_size("narrow")
    root = math.sqrt(total)
    any_space = pl.BlockSpec(memory_space=pl.ANY)
    vmem = pl.BlockSpec(memory_space=pltpu.VMEM)
    mixer = jnp.asarray(sylvester(INNER) / root, BF16)
    chunked = pltpu.VMEM((CHUNKS, GROUP, count), F32)
    dma = pltpu.SemaphoreType.DMA
    return pl.pallas_call(
        functools.partial(mix_kernel, total / sample_rows.shape[0], root),
        out_shape=(
            jax.ShapeDtypeStruct((cols, count), F32),
            jax.ShapeDtypeStruct((cols, cols), F32),
            jax.ShapeDtypeStruct((cols, count), F32),
        ),
        in_specs=[any_space, vmem, vmem, vmem],
        out_specs=(any_space, vmem, any_space),
        scratch_shapes=[chunked] * 9
        + [
            pltpu.VMEM((cols, count), F32),
            pltpu.VMEM((2 * cols, count), BF16),
            pltpu.VMEM((128, 128), F32),
            pltpu.VMEM((cols, 128), F32),
            pltpu.VMEM((N_Z, GROUP, 128), F32),
            pltpu.VMEM((GROUP, 128), F32),
            pltpu.VMEM((PLANE * N_CORE, GROUP, 128), F32),
            pltpu.VMEM((cols, 128), F32),
        ]
        + [dma((CHUNKS,))] * 2
        + [dma((count // 1024,))]
        + [dma((CHUNKS,))] * 10
        + [dma((1,))] * 6,
        compiler_params=pltpu.CompilerParams(
            collective_id=0, has_side_effects=True, vmem_limit_bytes=56 * 1024 * 1024
        ),
    )(panel, signs.reshape(1, count), sample_rows.reshape(-1, 128), mixer)


def solution(mesh):
    in_specs = (P(None, ("wide", "narrow")), P(("wide", "narrow")), P())
    out_specs = (P(None, ("wide", "narrow")), P(), P(None, ("wide", "narrow")))
    return jax.shard_map(body, mesh=mesh, in_specs=in_specs, out_specs=out_specs, check_vma=False)
```

time: 229 us -> 206 us (0.90)
  Pallas kernels: 225 us -> 198 us
  local copies, waits for them, and re-layouts: 2.94 us -> 7.29 us
    pallas_call x2 -> x1, Pallas kernels: 225 us -> 198 us  [body(): pl.pallas_call(functools.partial(mix_kernel, total / sample_rows.shape[0]...]
    unnamed x6 -> x7, local copies, waits for them, and re-layouts: 2.94 us -> 7.29 us
where the time goes in v2:
time: 206 us
  Pallas kernels  198 us (96%)
  local copies, waits for them, and re-layouts  7.29 us (4%)
    pallas_call x1, Pallas kernels, body(): pl.pallas_call(functools.partial(mix_kernel, total / sample_rows.shape[0]...  198 us
    unnamed x7, local copies, waits for them, and re-layouts  7.29 us

profile of v2, /device:TPU:1, one launch (start us, length us, event | category | flops | bytes accessed | tf_op | source)
XLA Modules:
  0.0 206.0 jit_solution(6787767081012349394)
XLA Ops:
  0.6 198.0 %shard_map.67 = (f32[64,16384]{1,0:T(8,128)}, f32[64,64]{1,0:T(8,128)}, f32[64,16384]{1,0:T(8,128)}) custom-call(f32[64,16384]{1,0:T(8,128)} %panel_ref.1, s32[1,16384]{1,0:T(1,128)} %bitcast.2, s32[128,128]{1,0:T(8,128)} %bitcast.3, bf16[256,256]{1,0:T(8,128)(2,1)} %constant.2.clone.h_ref), custom_call_target="tpu_custom_call" | custom-call | tf_op jit(solution)/shard_map/pallas_call | solution.py:379
  198.6 0.0 copy-start.1
  198.7 0.0 copy-start
  198.7 4.7 %copy.10 = f32[64,16384]{1,0:T(8,128)} copy(f32[64,16384]{1,0:T(8,128)} %get-tuple-element.6) | data formatting | bytes 8388608
  203.3 0.0 copy-done.1
  203.3 0.6 copy.11
  203.9 0.0 copy-done
  203.9 2.0 copy.12
Async XLA Ops:
  198.6 4.7 %copy-start.1 = (f32[64,64]{1,0:T(8,128)S(1)}, f32[64,64]{1,0:T(8,128)}, u32[]{:S(2)}) copy-start(f32[64,64]{1,0:T(8,128)} %get-tuple-element.7) | copy-start | bytes 49156
  198.7 5.3 %copy-start = (f32[64,16384]{1,0:T(8,128)S(1)}, f32[64,16384]{1,0:T(8,128)}, u32[]{:S(2)}) copy-start(f32[64,16384]{1,0:T(8,128)} %get-tuple-element.8) | copy-start | bytes 12582916

commit v3 on v2

--- a/solution.py
+++ b/solution.py
@@ -3,7 +3,6 @@
 
 import jax
 import jax.numpy as jnp
-import numpy as np
 from jax import lax
 from jax.experimental import pallas as pl
 from jax.experimental.pallas import tpu as pltpu
@@ -26,13 +25,6 @@
 INNER = 256
 
 
-def sylvester(order):
-    matrix = np.ones((1, 1), np.float32)
-    while matrix.shape[0] < order:
-        matrix = np.block([[matrix, matrix], [matrix, -matrix]])
-    return matrix
-
-
 def butterflies(parts):
     parts = list(parts)
     half = 1
@@ -54,10 +46,12 @@
 
 
 def mix_kernel(
-    scale, root, panel_ref, signs_ref, samples_ref, h_ref, mixed_ref, r_ref, precond_ref,
-    panel, s0, r1, s1, r2, s2, r3, e, s3, out, tw, weight, g_own, g_z, g_zsum, g_plane, gram,
-    in_sem, own_sem, out_sem, send1, recv1, send2, recv2, send3, recv3, send4, recv4,
-    send_core, recv_core, send_gz, recv_gz, send_gp, recv_gp, send_gg, recv_gg,
+    scale, root, panel_ref, signs_hbm, samples_hbm, mixed_ref, r_ref, out,
+    panel, signs_ref, samples_ref, h_ref, s0, r1, s1, r2, s2, r3, e, s3, tw, weight,
+    g_own, g_z, g_zsum, g_plane, g_psum, g_core, gram,
+    in_sem, own_sem, signs_sem, samples_sem, send1, recv1, send2, recv2, send3, recv3, send4, recv4,
+    send_core, recv_core, send_gz, recv_gz, send_gp, recv_gp, send_gc, recv_gc,
+    send_gg, recv_gg,
 ):
     wide = lax.axis_index("wide")
     z = lax.axis_index("narrow")
@@ -71,8 +65,7 @@
     xy_peers = [device(y + a, x + b, core, z) for a, b in xy_offsets]
     xy_index = [((y + a) % N_Y) * N_X + (x + b) % N_X for a, b in xy_offsets]
     sibling = device(y, x, core + 1, z)
-    crossed = [device(y + a, x + b, core + 1, z) for a, b in xy_offsets]
-    plane_peers = xy_peers + [sibling] + crossed
+    peers = z_peers + xy_peers + [sibling]
 
     def band(c):
         return pl.ds(pl.multiple_of(c * GROUP, GROUP), GROUP)
@@ -80,12 +73,21 @@
     def load(c):
         return pltpu.make_async_copy(panel_ref.at[band(c)], panel.at[c], in_sem.at[c])
 
-    for c in range(CHUNKS):
+    barrier = pltpu.get_barrier_semaphore()
+
+    def greet(some):
+        for peer in some:
+            pl.semaphore_signal(barrier, inc=1, device_id=peer, device_id_type=MESH)
+
+    load_signs = pltpu.make_async_copy(signs_hbm, signs_ref, signs_sem)
+    load_samples = pltpu.make_async_copy(samples_hbm, samples_ref, samples_sem)
+    greet(z_peers)
+    load_signs.start()
+    load(0).start()
+    greet(xy_peers + [sibling])
+    for c in range(1, CHUNKS):
         load(c).start()
-
-    barrier = pltpu.get_barrier_semaphore()
-    for peer in z_peers + plane_peers:
-        pl.semaphore_signal(barrier, inc=1, device_id=peer, device_id_type=MESH)
+    load_samples.start()
 
     def send(over_z, src, target, c, send_sem, recv_sem):
         size = Z_LEN if over_z else P_LEN
@@ -104,56 +106,24 @@
         part = ref.at[c, :, pl.ds(0, COUNT - (Z_LEN if over_z else P_LEN))]
         pltpu.make_async_copy(part, part, sem.at[c]).wait()
 
-    def combine(over_z, own, got, out, c):
-        size = Z_LEN if over_z else P_LEN
-        n = N_Z if over_z else PLANE
-        mine = lanes((z if over_z else q) * size, size)
-        got[c, :, mine] = own[c, :, mine]
-        step = 4096 // n
-
-        def part(i, carry):
-            places = [lanes(p * size + i * step, step) for p in range(n)]
-            values = butterflies([got[c, :, place] for place in places])
-            for place, value in zip(places, values):
-                out[c, :, place] = value
-            return carry
-
-        lax.fori_loop(0, size // step, part, 0)
-
     def mix(c):
         load(c).wait()
 
-        def slab(i, carry):
-            place = lanes(i * 1024, 1024)
-            values = panel[c, :, place] * signs_ref[:, place].astype(F32)
-            low = values - values.astype(BF16).astype(F32)
-            rows = []
-            for b in range(1024 // INNER):
-                rows += [values[:, b * INNER:(b + 1) * INNER], low[:, b * INNER:(b + 1) * INNER]]
-            stacked = jnp.concatenate(rows, axis=0).astype(BF16)
-            done = jnp.dot(stacked, h_ref[...], preferred_element_type=F32)
-            parts = [
-                done[16 * b:16 * b + 8] + done[16 * b + 8:16 * b + 16] for b in range(1024 // INNER)
-            ]
-            s0[c, :, place] = jnp.concatenate(butterflies(parts), axis=1)
-            return carry
-
-        lax.fori_loop(0, COUNT // 1024, slab, 0)
-
         def part(i, carry):
-            places = [lanes(p * 1024 + i * 256, 256) for p in range(16)]
-            values = butterflies([s0[c, :, place] for place in places])
-            for place, value in zip(places, values):
+            places = [lanes(p * Z_LEN + i * 512, 512) for p in range(N_Z)]
+            values = [panel[c, :, place] * signs_ref[:, place].astype(F32) for place in places]
+            for place, value in zip(places, butterflies(values)):
                 s0[c, :, place] = value
             return carry
 
-        lax.fori_loop(0, 4, part, 0)
+        lax.fori_loop(0, Z_LEN // 512, part, 0)
 
     def send_z(c):
         send(True, s0, lambda place: r1.at[c, :, place], c, send1, recv1)
 
+    load_signs.wait()
     mix(0)
-    pl.semaphore_wait(barrier, len(z_peers) + len(plane_peers))
+    pl.semaphore_wait(barrier, len(peers))
     send_z(0)
 
     def begin(c, carry):
@@ -163,6 +133,7 @@
 
     lax.fori_loop(1, CHUNKS, begin, 0)
 
+    load_samples.wait()
     weight[...] = jnp.zeros_like(weight)
 
     def mark(i, carry):
@@ -189,14 +160,56 @@
 
     lax.fori_loop(0, 16, mark, 0)
 
+    common = jnp.bitwise_and(
+        lax.broadcasted_iota(jnp.int32, (INNER, INNER), 0),
+        lax.broadcasted_iota(jnp.int32, (INNER, INNER), 1),
+    )
+    for shift in (4, 2, 1):
+        common = jnp.bitwise_xor(common, jnp.right_shift(common, shift))
+    h_ref[...] = jnp.where(jnp.bitwise_and(common, 1) == 0, 1.0 / root, -1.0 / root).astype(BF16)
+
     def plane_out(c):
         await_bytes(True, r1, c, recv1)
-        combine(True, s0, r1, s1, c)
+        mine = lanes(z * Z_LEN, Z_LEN)
+        r1[c, :, mine] = s0[c, :, mine]
+
+        def inner(i, carry):
+            places = [lanes(p * Z_LEN + i * INNER, INNER) for p in range(N_Z)]
+            values = butterflies([r1[c, :, place] for place in places])
+            rows = []
+            for value in values:
+                rows += [value, value - value.astype(BF16).astype(F32)]
+            stacked = jnp.concatenate(rows, axis=0).astype(BF16)
+            done = jnp.dot(stacked, h_ref[...], preferred_element_type=F32)
+            for p, place in enumerate(places):
+                s1[c, :, place] = done[16 * p:16 * p + 8] + done[16 * p + 8:16 * p + 16]
+            return carry
+
+        lax.fori_loop(0, Z_LEN // INNER, inner, 0)
+
+        def outer(p, carry):
+            places = [lanes(p * Z_LEN + i * INNER, INNER) for i in range(Z_LEN // INNER)]
+            values = butterflies([s1[c, :, place] for place in places])
+            for place, value in zip(places, values):
+                s1[c, :, place] = value
+            return carry
+
+        lax.fori_loop(0, N_Z, outer, 0)
         send(False, s1, lambda place: r2.at[c, :, place], c, send2, recv2)
 
     def plane_back(c):
         await_bytes(False, r2, c, recv2)
-        combine(False, s1, r2, s2, c)
+        mine = lanes(q * P_LEN, P_LEN)
+        r2[c, :, mine] = s1[c, :, mine]
+
+        def part(i, carry):
+            places = [lanes(p * P_LEN + i * 256, 256) for p in range(PLANE)]
+            values = butterflies([r2[c, :, place] for place in places])
+            for place, value in zip(places, values):
+                s2[c, :, place] = value
+            return carry
+
+        lax.fori_loop(0, P_LEN // 256, part, 0)
         send(False, s2, lambda place: r3.at[c, :, place], c, send3, recv3)
 
     def core_copy(c):
@@ -285,17 +298,22 @@
     others = g_z.at[pl.ds(0, N_Z - 1)]
     pltpu.make_async_copy(others, others, recv_gz.at[0]).wait()
     g_zsum[...] = functools.reduce(lambda a, b: a + b, [g_z[k] for k in range(N_Z)])
-    for peer in plane_peers:
+    for peer in xy_peers:
         pltpu.make_async_remote_copy(
-            src_ref=g_zsum, dst_ref=g_plane.at[wide], send_sem=send_gp.at[0],
+            src_ref=g_zsum, dst_ref=g_plane.at[q], send_sem=send_gp.at[0],
             recv_sem=recv_gp.at[0], device_id=peer, device_id_type=MESH,
         ).start()
-    g_plane[wide] = g_zsum[...]
-    planes = g_plane.at[pl.ds(0, PLANE * N_CORE - 1)]
+    g_plane[q] = g_zsum[...]
+    planes = g_plane.at[pl.ds(0, PLANE - 1)]
     pltpu.make_async_copy(planes, planes, recv_gp.at[0]).wait()
-    gram[band(z)] = functools.reduce(
-        lambda a, b: a + b, [g_plane[k] for k in range(PLANE * N_CORE)]
+    g_psum[...] = functools.reduce(lambda a, b: a + b, [g_plane[k] for k in range(PLANE)])
+    to_sibling = pltpu.make_async_remote_copy(
+        src_ref=g_psum, dst_ref=g_core, send_sem=send_gc.at[0],
+        recv_sem=recv_gc.at[0], device_id=sibling, device_id_type=MESH,
     )
+    to_sibling.start()
+    to_sibling.wait()
+    gram[band(z)] = g_psum[...] + g_core[...]
     for peer in z_peers:
         pltpu.make_async_remote_copy(
             src_ref=gram.at[band(z)], dst_ref=gram.at[band(z)], send_sem=send_gg.at[0],
@@ -327,10 +345,6 @@
     low = (inverse - high.astype(F32)).astype(BF16)
     left = jnp.concatenate([high, low, high], axis=1)
 
-    def tile(i):
-        place = lanes(i * 1024, 1024)
-        return pltpu.make_async_copy(out.at[:, place], precond_ref.at[:, place], out_sem.at[i])
-
     def multiply(i, carry):
         place = lanes(i * 1024, 1024)
         values = jnp.concatenate([panel[c, :, place] for c in range(CHUNKS)], axis=0)
@@ -338,7 +352,6 @@
         values_low = (values - values_high.astype(F32)).astype(BF16)
         right = jnp.concatenate([values_high, values_high, values_low], axis=0)
         out[:, place] = jnp.dot(left, right, preferred_element_type=F32)
-        tile(i).start()
         return carry
 
     lax.fori_loop(0, COUNT // 1024, multiply, 0)
@@ -347,24 +360,32 @@
     pltpu.make_async_copy(planes, planes, send_gp.at[0]).wait()
     pltpu.make_async_copy(bands, bands, send_gg.at[0]).wait()
 
-    def drain(i, carry):
-        tile(i).wait()
-        return carry
-
-    lax.fori_loop(0, COUNT // 1024, drain, 0)
-
-    def arrived(c, carry):
+    def left_all(c, carry):
         await_bytes(True, s0, c, send1)
         await_bytes(False, s1, c, send2)
         await_bytes(False, s2, c, send3)
         core_copy(c).wait_send()
         keep(c).wait()
+        return carry
+
+    lax.fori_loop(0, CHUNKS, left_all, 0)
+
+    def arrived(c, carry):
         await_bytes(True, s3, c, send4)
         part = mixed_ref.at[band(c), pl.ds(0, COUNT - Z_LEN)]
         pltpu.make_async_copy(part, part, recv4.at[c]).wait()
         return carry
 
     lax.fori_loop(0, CHUNKS, arrived, 0)
+
+
+def move_kernel(mixed_in, r_in, precond_in, mixed_ref, r_ref, precond_ref, sem):
+    pairs = [(mixed_in, mixed_ref), (precond_in, precond_ref), (r_in, r_ref)]
+    copies = [pltpu.make_async_copy(a, b, sem.at[i]) for i, (a, b) in enumerate(pairs)]
+    for copy in copies:
+        copy.start()
+    for copy in copies:
+        copy.wait()
 
 
 def body(panel, signs, sample_rows):
@@ -373,37 +394,50 @@
     root = math.sqrt(total)
     any_space = pl.BlockSpec(memory_space=pl.ANY)
     vmem = pl.BlockSpec(memory_space=pltpu.VMEM)
-    mixer = jnp.asarray(sylvester(INNER) / root, BF16)
     chunked = pltpu.VMEM((CHUNKS, GROUP, count), F32)
+    small = pltpu.VMEM((GROUP, 128), F32)
     dma = pltpu.SemaphoreType.DMA
-    return pl.pallas_call(
+    shapes = [(cols, count), (cols, cols), (cols, count)]
+    arguments = (panel, signs.reshape(1, count), sample_rows.reshape(-1, 128))
+    results = pl.pallas_call(
         functools.partial(mix_kernel, total / sample_rows.shape[0], root),
-        out_shape=(
-            jax.ShapeDtypeStruct((cols, count), F32),
-            jax.ShapeDtypeStruct((cols, cols), F32),
-            jax.ShapeDtypeStruct((cols, count), F32),
-        ),
-        in_specs=[any_space, vmem, vmem, vmem],
-        out_specs=(any_space, vmem, any_space),
-        scratch_shapes=[chunked] * 9
+        out_shape=tuple(pltpu.VMEM(shape, F32) for shape in shapes),
+        in_specs=[any_space] * 3,
+        out_specs=(vmem,) * 3,
+        scratch_shapes=[
+            chunked,
+            pltpu.VMEM((1, count), jnp.int32),
+            pltpu.VMEM((128, 128), jnp.int32),
+            pltpu.VMEM((INNER, INNER), BF16),
+        ]
+        + [chunked] * 8
         + [
-            pltpu.VMEM((cols, count), F32),
             pltpu.VMEM((2 * cols, count), BF16),
             pltpu.VMEM((128, 128), F32),
             pltpu.VMEM((cols, 128), F32),
             pltpu.VMEM((N_Z, GROUP, 128), F32),
-            pltpu.VMEM((GROUP, 128), F32),
-            pltpu.VMEM((PLANE * N_CORE, GROUP, 128), F32),
+            small,
+            pltpu.VMEM((PLANE, GROUP, 128), F32),
+            small,
+            small,
             pltpu.VMEM((cols, 128), F32),
         ]
         + [dma((CHUNKS,))] * 2
-        + [dma((count // 1024,))]
+        + [dma, dma]
         + [dma((CHUNKS,))] * 10
-        + [dma((1,))] * 6,
+        + [dma((1,))] * 8,
         compiler_params=pltpu.CompilerParams(
-            collective_id=0, has_side_effects=True, vmem_limit_bytes=56 * 1024 * 1024
+            collective_id=0, has_side_effects=True, vmem_limit_bytes=44 * 1024 * 1024
         ),
-    )(panel, signs.reshape(1, count), sample_rows.reshape(-1, 128), mixer)
+    )(*(pltpu.with_memory_space_constraint(one, pltpu.HBM) for one in arguments))
+    return pl.pallas_call(
+        move_kernel,
+        out_shape=tuple(jax.ShapeDtypeStruct(shape, F32) for shape in shapes),
+        in_specs=[any_space] * 3,
+        out_specs=(any_space,) * 3,
+        scratch_shapes=[dma((3,))],
+        compiler_params=pltpu.CompilerParams(vmem_limit_bytes=1024 * 1024),
+    )(*results)
 
 
 def solution(mesh):

time: 206 us -> 201 us (0.976)
  local copies, waits for them, and re-layouts: 7.29 us -> 0 us
    unnamed x7 -> x0, local copies, waits for them, and re-layouts: 7.29 us -> none
    pallas_call x0 -> x1, Pallas kernels: none -> 3.42 us  [body(): pl.pallas_call(move_kernel, out_shape=tuple((jax.ShapeDtypeStruct(shape,...]
where the time goes in v3:
time: 201 us
  Pallas kernels  200 us (100%)
    pallas_call x1, Pallas kernels, body(): pl.pallas_call(functools.partial(mix_kernel, total / sample_rows.shape[0]...  197 us

profile of v3, /device:TPU:1, one launch (start us, length us, event | category | flops | bytes accessed | tf_op | source)
XLA Modules:
  0.0 200.8 jit_solution(12278032304118319735)
XLA Ops:
  0.6 196.7 %shard_map.58 = (f32[64,16384]{1,0:T(8,128)S(1)}, f32[64,64]{1,0:T(8,128)S(1)}, f32[64,16384]{1,0:T(8,128)S(1)}) custom-call(f32[64,16384]{1,0:T(8,128)} %panel_ref.1, s32[1,16384]{1,0:T(1,128)} %bitcast.2, s32[128,128]{1,0:T(8,128)} %bitcast.3), custom_call_target="tpu_custom_call" | custom-call | tf_op jit(solution)/shard_map/pallas_call | solution.py:402
  197.3 3.4 %shard_map.59 = (f32[64,16384]{1,0:T(8,128)}, f32[64,64]{1,0:T(8,128)}, f32[64,16384]{1,0:T(8,128)}) custom-call(f32[64,16384]{1,0:T(8,128)S(1)} %get-tuple-element.6.mixed_in, f32[64,64]{1,0:T(8,128)S(1)} %get-tuple-element.7.r_in, f32[64,16384]{1,0:T(8,128)S(1)} %get-tuple-element.8.precond_in), custom_call_target="tpu_custom_call" | custom-call | tf_op jit(solution)/shard_map/pallas_call | solution.py:433

commit v4 on v3

--- a/solution.py
+++ b/solution.py
@@ -19,7 +19,8 @@
 COUNT = 16384
 GROUP = 8
 CHUNKS = COLS // GROUP
-AHEAD = 4
+DESK, TELLER = 6, 5
+AHEAD = 3
 Z_LEN = COUNT // N_Z
 P_LEN = COUNT // PLANE
 INNER = 256
@@ -51,7 +52,7 @@
     g_own, g_z, g_zsum, g_plane, g_psum, g_core, gram,
     in_sem, own_sem, signs_sem, samples_sem, send1, recv1, send2, recv2, send3, recv3, send4, recv4,
     send_core, recv_core, send_gz, recv_gz, send_gp, recv_gp, send_gc, recv_gc,
-    send_gg, recv_gg,
+    send_gg, recv_gg, ring_sem, plane_sem,
 ):
     wide = lax.axis_index("wide")
     z = lax.axis_index("narrow")
@@ -65,7 +66,6 @@
     xy_peers = [device(y + a, x + b, core, z) for a, b in xy_offsets]
     xy_index = [((y + a) % N_Y) * N_X + (x + b) % N_X for a, b in xy_offsets]
     sibling = device(y, x, core + 1, z)
-    peers = z_peers + xy_peers + [sibling]
 
     def band(c):
         return pl.ds(pl.multiple_of(c * GROUP, GROUP), GROUP)
@@ -81,10 +81,18 @@
 
     load_signs = pltpu.make_async_copy(signs_hbm, signs_ref, signs_sem)
     load_samples = pltpu.make_async_copy(samples_hbm, samples_ref, samples_sem)
-    greet(z_peers)
+    for d in range(1, N_Z):
+        pl.when((z + d) % N_Z != DESK)(functools.partial(greet, [z_peers[d - 1]]))
     load_signs.start()
     load(0).start()
-    greet(xy_peers + [sibling])
+
+    @pl.when(z == TELLER)
+    def _():
+        pl.semaphore_wait(barrier, N_Z - 1)
+        pl.semaphore_signal(
+            ring_sem, inc=1, device_id=device(y, x, core, DESK), device_id_type=MESH
+        )
+
     for c in range(1, CHUNKS):
         load(c).start()
     load_samples.start()
@@ -123,8 +131,21 @@
 
     load_signs.wait()
     mix(0)
-    pl.semaphore_wait(barrier, len(peers))
+
+    @pl.when((z != TELLER) & (z != DESK))
+    def _():
+        pl.semaphore_wait(barrier, N_Z - 1)
+
+    @pl.when(z == DESK)
+    def _():
+        pl.semaphore_wait(ring_sem, 1)
+
     send_z(0)
+
+    @pl.when(z == DESK)
+    def _():
+        greet(xy_peers + [sibling])
+
 
     def begin(c, carry):
         mix(c)
@@ -160,6 +181,16 @@
 
     lax.fori_loop(0, 16, mark, 0)
 
+    @pl.when(z == DESK)
+    def _():
+        pl.semaphore_wait(barrier, PLANE)
+        for peer in z_peers:
+            pl.semaphore_signal(plane_sem, inc=1, device_id=peer, device_id_type=MESH)
+
+    @pl.when(z != DESK)
+    def _():
+        pl.semaphore_wait(plane_sem, 1)
+
     common = jnp.bitwise_and(
         lax.broadcasted_iota(jnp.int32, (INNER, INNER), 0),
         lax.broadcasted_iota(jnp.int32, (INNER, INNER), 1),
@@ -294,6 +325,7 @@
             recv_sem=recv_gz.at[0], device_id=peer, device_id_type=MESH,
         ).start()
     z_back(AHEAD, 0)
+    z_back(AHEAD + 1, 0)
     g_z[z] = g_own[band(z)]
     others = g_z.at[pl.ds(0, N_Z - 1)]
     pltpu.make_async_copy(others, others, recv_gz.at[0]).wait()
@@ -319,7 +351,7 @@
             src_ref=gram.at[band(z)], dst_ref=gram.at[band(z)], send_sem=send_gg.at[0],
             recv_sem=recv_gg.at[0], device_id=peer, device_id_type=MESH,
         ).start()
-    lax.fori_loop(AHEAD + 1, CHUNKS, z_back, 0)
+    lax.fori_loop(AHEAD + 2, CHUNKS, z_back, 0)
     bands = gram.at[pl.ds(0, COLS - GROUP)]
     pltpu.make_async_copy(bands, bands, recv_gg.at[0]).wait()
 
@@ -425,7 +457,8 @@
         + [dma((CHUNKS,))] * 2
         + [dma, dma]
         + [dma((CHUNKS,))] * 10
-        + [dma((1,))] * 8,
+        + [dma((1,))] * 8
+        + [pltpu.SemaphoreType.REGULAR] * 2,
         compiler_params=pltpu.CompilerParams(
             collective_id=0, has_side_effects=True, vmem_limit_bytes=44 * 1024 * 1024
         ),

time: 201 us -> 196 us (0.975)
  Pallas kernels: 200 us -> 195 us
    pallas_call x1, Pallas kernels: 197 us -> 191 us  [body(): pl.pallas_call(functools.partial(mix_kernel, total / sample_rows.shape[0]...]
where the time goes in v4:
time: 196 us
  Pallas kernels  195 us (99%)
    pallas_call x1, Pallas kernels, body(): pl.pallas_call(functools.partial(mix_kernel, total / sample_rows.shape[0]...  191 us

profile of v4, /device:TPU:1, one launch (start us, length us, event | category | flops | bytes accessed | tf_op | source)
XLA Modules:
  0.0 195.5 jit_solution(16134292205412785358)
XLA Ops:
  0.6 191.4 %shard_map.58 = (f32[64,16384]{1,0:T(8,128)S(1)}, f32[64,64]{1,0:T(8,128)S(1)}, f32[64,16384]{1,0:T(8,128)S(1)}) custom-call(f32[64,16384]{1,0:T(8,128)} %panel_ref.1, s32[1,16384]{1,0:T(1,128)} %bitcast.2, s32[128,128]{1,0:T(8,128)} %bitcast.3), custom_call_target="tpu_custom_call" | custom-call | tf_op jit(solution)/shard_map/pallas_call | solution.py:434
  192.1 3.4 %shard_map.59 = (f32[64,16384]{1,0:T(8,128)}, f32[64,64]{1,0:T(8,128)}, f32[64,16384]{1,0:T(8,128)}) custom-call(f32[64,16384]{1,0:T(8,128)S(1)} %get-tuple-element.6.mixed_in, f32[64,64]{1,0:T(8,128)S(1)} %get-tuple-element.7.r_in, f32[64,16384]{1,0:T(8,128)S(1)} %get-tuple-element.8.precond_in), custom_call_target="tpu_custom_call" | custom-call | tf_op jit(solution)/shard_map/pallas_call | solution.py:466

commit v5 on v4

--- a/solution.py
+++ b/solution.py
@@ -20,7 +20,7 @@
 GROUP = 8
 CHUNKS = COLS // GROUP
 DESK, TELLER = 6, 5
-AHEAD = 3
+AHEAD = 4
 Z_LEN = COUNT // N_Z
 P_LEN = COUNT // PLANE
 INNER = 256
@@ -36,6 +36,13 @@
                 parts[low], parts[low | half] = first + second, first - second
         half *= 2
     return parts
+
+
+def pieces(values):
+    high = values.astype(BF16).astype(F32)
+    rest = values - high
+    middle = rest.astype(BF16).astype(F32)
+    return [high, middle, rest - middle]
 
 
 def lanes(start, size):
@@ -209,11 +216,12 @@
             values = butterflies([r1[c, :, place] for place in places])
             rows = []
             for value in values:
-                rows += [value, value - value.astype(BF16).astype(F32)]
+                rows += pieces(value)
             stacked = jnp.concatenate(rows, axis=0).astype(BF16)
             done = jnp.dot(stacked, h_ref[...], preferred_element_type=F32)
             for p, place in enumerate(places):
-                s1[c, :, place] = done[16 * p:16 * p + 8] + done[16 * p + 8:16 * p + 16]
+                part = done[24 * p:24 * p + 24]
+                s1[c, :, place] = part[:8] + (part[8:16] + part[16:])
             return carry
 
         lax.fori_loop(0, Z_LEN // INNER, inner, 0)
@@ -271,9 +279,8 @@
             rows = weight[pl.ds(pl.multiple_of(i * 8, 8), 8), :]
             mask = jnp.concatenate([rows[k:k + 1] for k in range(8)], axis=1)
             values = values * mask
-            low = values - values.astype(BF16).astype(F32)
-            both = jnp.concatenate([values, low], axis=0).astype(BF16)
-            tw[pl.ds(pl.multiple_of(c * 16, 16), 16), place] = both
+            rows = jnp.concatenate(pieces(values) + [jnp.zeros_like(values)], axis=0).astype(BF16)
+            tw[pl.ds(pl.multiple_of(c * 32, 32), 32), place] = rows
             return carry
 
         lax.fori_loop(0, COUNT // 1024, slab, 0)
@@ -310,13 +317,15 @@
         part = tw[:, lanes(i * 2048, 2048)]
         return total + lax.dot_general(part, part, NT, preferred_element_type=F32)
 
-    total = lax.fori_loop(0, COUNT // 2048, product, jnp.zeros((128, 128), F32))
-    rows = jnp.concatenate(
-        [total[16 * c:16 * c + 8] + total[16 * c + 8:16 * c + 16] for c in range(CHUNKS)], axis=0
-    )
-    lane = lax.broadcasted_iota(jnp.int32, (128, 128), 0)
-    column = lax.broadcasted_iota(jnp.int32, (128, 128), 1)
-    chosen = jnp.where((lane // 16) * 8 + lane % 8 == column, 1.0, 0.0)
+    total = lax.fori_loop(0, COUNT // 2048, product, jnp.zeros((256, 256), F32))
+    rows = []
+    for c in range(CHUNKS):
+        part = total[32 * c:32 * c + 24]
+        rows.append(part[:8] + (part[8:16] + part[16:]))
+    rows = jnp.concatenate(rows, axis=0)
+    lane = lax.broadcasted_iota(jnp.int32, (256, 128), 0)
+    column = lax.broadcasted_iota(jnp.int32, (256, 128), 1)
+    chosen = jnp.where((lane // 32) * 8 + lane % 8 == column, 1.0, 0.0)
     g_own[...] = jnp.dot(rows, chosen, precision=lax.Precision.HIGHEST, preferred_element_type=F32)
 
     for peer, place in zip(z_peers, z_index):
@@ -373,16 +382,14 @@
     square = done[:, :COLS]
     r_ref[...] = jnp.where(row[:, :COLS] <= column[:, :COLS], square * (1.0 / root), 0.0)
     inverse = done[:, COLS:] * root
-    high = inverse.astype(BF16)
-    low = (inverse - high.astype(F32)).astype(BF16)
-    left = jnp.concatenate([high, low, high], axis=1)
+    high, middle, low = [piece.astype(BF16) for piece in pieces(inverse)]
+    left = jnp.concatenate([high, high, middle, high, middle, low], axis=1)
 
     def multiply(i, carry):
         place = lanes(i * 1024, 1024)
         values = jnp.concatenate([panel[c, :, place] for c in range(CHUNKS)], axis=0)
-        values_high = values.astype(BF16)
-        values_low = (values - values_high.astype(F32)).astype(BF16)
-        right = jnp.concatenate([values_high, values_high, values_low], axis=0)
+        high, middle, low = [piece.astype(BF16) for piece in pieces(values)]
+        right = jnp.concatenate([high, middle, high, low, middle, high], axis=0)
         out[:, place] = jnp.dot(left, right, preferred_element_type=F32)
         return carry
 
@@ -444,7 +451,7 @@
         ]
         + [chunked] * 8
         + [
-            pltpu.VMEM((2 * cols, count), BF16),
+            pltpu.VMEM((4 * cols, count), BF16),
             pltpu.VMEM((128, 128), F32),
             pltpu.VMEM((cols, 128), F32),
             pltpu.VMEM((N_Z, GROUP, 128), F32),
@@ -460,7 +467,7 @@
         + [dma((1,))] * 8
         + [pltpu.SemaphoreType.REGULAR] * 2,
         compiler_params=pltpu.CompilerParams(
-            collective_id=0, has_side_effects=True, vmem_limit_bytes=44 * 1024 * 1024
+            collective_id=0, has_side_effects=True, vmem_limit_bytes=48 * 1024 * 1024
         ),
     )(*(pltpu.with_memory_space_constraint(one, pltpu.HBM) for one in arguments))
     return pl.pallas_call(

time: 196 us -> 196 us (level)
  no operation moved by 1% of the time
where the time goes in v5:
time: 196 us
  Pallas kernels  195 us (99%)
    pallas_call x1, Pallas kernels, body(): pl.pallas_call(functools.partial(mix_kernel, total / sample_rows.shape[0]...  191 us

profile of v5, /device:TPU:1, one launch (start us, length us, event | category | flops | bytes accessed | tf_op | source)
XLA Modules:
  0.0 195.5 jit_solution(17691642303484851770)
XLA Ops:
  0.6 191.5 %shard_map.58 = (f32[64,16384]{1,0:T(8,128)S(1)}, f32[64,64]{1,0:T(8,128)S(1)}, f32[64,16384]{1,0:T(8,128)S(1)}) custom-call(f32[64,16384]{1,0:T(8,128)} %panel_ref.1, s32[1,16384]{1,0:T(1,128)} %bitcast.2, s32[128,128]{1,0:T(8,128)} %bitcast.3), custom_call_target="tpu_custom_call" | custom-call | tf_op jit(solution)/shard_map/pallas_call | solution.py:441
  192.1 3.4 %shard_map.59 = (f32[64,16384]{1,0:T(8,128)}, f32[64,64]{1,0:T(8,128)}, f32[64,16384]{1,0:T(8,128)}) custom-call(f32[64,16384]{1,0:T(8,128)S(1)} %get-tuple-element.6.mixed_in, f32[64,64]{1,0:T(8,128)S(1)} %get-tuple-element.7.r_in, f32[64,16384]{1,0:T(8,128)S(1)} %get-tuple-element.8.precond_in), custom_call_target="tpu_custom_call" | custom-call | tf_op jit(solution)/shard_map/pallas_call | solution.py:473

commit v6 on v5

--- a/solution.py
+++ b/solution.py
@@ -56,7 +56,7 @@
 def mix_kernel(
     scale, root, panel_ref, signs_hbm, samples_hbm, mixed_ref, r_ref, out,
     panel, signs_ref, samples_ref, h_ref, s0, r1, s1, r2, s2, r3, e, s3, tw, weight,
-    g_own, g_z, g_zsum, g_plane, g_psum, g_core, gram,
+    g_own, g_z, g_zsum, g_plane, g_core, gram,
     in_sem, own_sem, signs_sem, samples_sem, send1, recv1, send2, recv2, send3, recv3, send4, recv4,
     send_core, recv_core, send_gz, recv_gz, send_gp, recv_gp, send_gc, recv_gc,
     send_gg, recv_gg, ring_sem, plane_sem,
@@ -328,41 +328,62 @@
     chosen = jnp.where((lane // 32) * 8 + lane % 8 == column, 1.0, 0.0)
     g_own[...] = jnp.dot(rows, chosen, precision=lax.Precision.HIGHEST, preferred_element_type=F32)
 
-    for peer, place in zip(z_peers, z_index):
-        pltpu.make_async_remote_copy(
-            src_ref=g_own.at[band(place)], dst_ref=g_z.at[z], send_sem=send_gz.at[0],
-            recv_sem=recv_gz.at[0], device_id=peer, device_id_type=MESH,
-        ).start()
+    def to_sibling(src, dst, i):
+        return pltpu.make_async_remote_copy(
+            src_ref=src, dst_ref=dst, send_sem=send_gc.at[i], recv_sem=recv_gc.at[i],
+            device_id=sibling, device_id_type=MESH,
+        )
+
+    others = g_z.at[pl.ds(0, N_Z - 1)]
+    planes = g_plane.at[pl.ds(0, PLANE - 1)]
+    bands = gram.at[pl.ds(0, COLS - GROUP)]
+
+    @pl.when(core == 1)
+    def _():
+        to_sibling(g_own, g_core, 0).start()
+
+    @pl.when(core == 0)
+    def _():
+        to_sibling(g_own, g_core, 0).wait_recv()
+        g_own[...] += g_core[...]
+        for peer, place in zip(z_peers, z_index):
+            pltpu.make_async_remote_copy(
+                src_ref=g_own.at[band(place)], dst_ref=g_z.at[z], send_sem=send_gz.at[0],
+                recv_sem=recv_gz.at[0], device_id=peer, device_id_type=MESH,
+            ).start()
+
     z_back(AHEAD, 0)
     z_back(AHEAD + 1, 0)
-    g_z[z] = g_own[band(z)]
-    others = g_z.at[pl.ds(0, N_Z - 1)]
-    pltpu.make_async_copy(others, others, recv_gz.at[0]).wait()
-    g_zsum[...] = functools.reduce(lambda a, b: a + b, [g_z[k] for k in range(N_Z)])
-    for peer in xy_peers:
-        pltpu.make_async_remote_copy(
-            src_ref=g_zsum, dst_ref=g_plane.at[q], send_sem=send_gp.at[0],
-            recv_sem=recv_gp.at[0], device_id=peer, device_id_type=MESH,
-        ).start()
-    g_plane[q] = g_zsum[...]
-    planes = g_plane.at[pl.ds(0, PLANE - 1)]
-    pltpu.make_async_copy(planes, planes, recv_gp.at[0]).wait()
-    g_psum[...] = functools.reduce(lambda a, b: a + b, [g_plane[k] for k in range(PLANE)])
-    to_sibling = pltpu.make_async_remote_copy(
-        src_ref=g_psum, dst_ref=g_core, send_sem=send_gc.at[0],
-        recv_sem=recv_gc.at[0], device_id=sibling, device_id_type=MESH,
-    )
-    to_sibling.start()
-    to_sibling.wait()
-    gram[band(z)] = g_psum[...] + g_core[...]
-    for peer in z_peers:
-        pltpu.make_async_remote_copy(
-            src_ref=gram.at[band(z)], dst_ref=gram.at[band(z)], send_sem=send_gg.at[0],
-            recv_sem=recv_gg.at[0], device_id=peer, device_id_type=MESH,
-        ).start()
+
+    @pl.when(core == 0)
+    def _():
+        g_z[z] = g_own[band(z)]
+        pltpu.make_async_copy(others, others, recv_gz.at[0]).wait()
+        g_zsum[...] = functools.reduce(lambda a, b: a + b, [g_z[k] for k in range(N_Z)])
+        for peer in xy_peers:
+            pltpu.make_async_remote_copy(
+                src_ref=g_zsum, dst_ref=g_plane.at[q], send_sem=send_gp.at[0],
+                recv_sem=recv_gp.at[0], device_id=peer, device_id_type=MESH,
+            ).start()
+        g_plane[q] = g_zsum[...]
+        pltpu.make_async_copy(planes, planes, recv_gp.at[0]).wait()
+        gram[band(z)] = functools.reduce(lambda a, b: a + b, [g_plane[k] for k in range(PLANE)])
+        for peer in z_peers:
+            pltpu.make_async_remote_copy(
+                src_ref=gram.at[band(z)], dst_ref=gram.at[band(z)], send_sem=send_gg.at[0],
+                recv_sem=recv_gg.at[0], device_id=peer, device_id_type=MESH,
+            ).start()
+
     lax.fori_loop(AHEAD + 2, CHUNKS, z_back, 0)
-    bands = gram.at[pl.ds(0, COLS - GROUP)]
-    pltpu.make_async_copy(bands, bands, recv_gg.at[0]).wait()
+
+    @pl.when(core == 0)
+    def _():
+        pltpu.make_async_copy(bands, bands, recv_gg.at[0]).wait()
+        to_sibling(gram, gram, 1).start()
+
+    @pl.when(core == 1)
+    def _():
+        to_sibling(gram, gram, 1).wait_recv()
 
     row = lax.broadcasted_iota(jnp.int32, (COLS, 2 * COLS), 0)
     column = lax.broadcasted_iota(jnp.int32, (COLS, 2 * COLS), 1)
@@ -395,9 +416,17 @@
 
     lax.fori_loop(0, COUNT // 1024, multiply, 0)
 
-    pltpu.make_async_copy(others, others, send_gz.at[0]).wait()
-    pltpu.make_async_copy(planes, planes, send_gp.at[0]).wait()
-    pltpu.make_async_copy(bands, bands, send_gg.at[0]).wait()
+    @pl.when(core == 0)
+    def _():
+        pltpu.make_async_copy(others, others, send_gz.at[0]).wait()
+        pltpu.make_async_copy(planes, planes, send_gp.at[0]).wait()
+        pltpu.make_async_copy(bands, bands, send_gg.at[0]).wait()
+        to_sibling(gram, gram, 1).wait_send()
+
+    @pl.when(core == 1)
+    def _():
+        to_sibling(g_own, g_core, 0).wait_send()
+
 
     def left_all(c, carry):
         await_bytes(True, s0, c, send1)
@@ -457,14 +486,15 @@
             pltpu.VMEM((N_Z, GROUP, 128), F32),
             small,
             pltpu.VMEM((PLANE, GROUP, 128), F32),
-            small,
-            small,
+            pltpu.VMEM((cols, 128), F32),
             pltpu.VMEM((cols, 128), F32),
         ]
         + [dma((CHUNKS,))] * 2
         + [dma, dma]
         + [dma((CHUNKS,))] * 10
-        + [dma((1,))] * 8
+        + [dma((1,))] * 4
+        + [dma((2,))] * 2
+        + [dma((1,))] * 2
         + [pltpu.SemaphoreType.REGULAR] * 2,
         compiler_params=pltpu.CompilerParams(
             collective_id=0, has_side_effects=True, vmem_limit_bytes=48 * 1024 * 1024

time: 196 us -> 195 us (level)
  no operation moved by 1% of the time
where the time goes in v6:
time: 195 us; the launch traced here: 194 us
  Pallas kernels  194 us (99%)
    pallas_call x1, Pallas kernels, body(): pl.pallas_call(functools.partial(mix_kernel, total / sample_rows.shape[0]...  190 us

profile of v6, /device:TPU:1, one launch (start us, length us, event | category | flops | bytes accessed | tf_op | source)
XLA Modules:
  0.0 194.2 jit_solution(14445858224902162220)
XLA Ops:
  0.6 190.2 %shard_map.58 = (f32[64,16384]{1,0:T(8,128)S(1)}, f32[64,64]{1,0:T(8,128)S(1)}, f32[64,16384]{1,0:T(8,128)S(1)}) custom-call(f32[64,16384]{1,0:T(8,128)} %panel_ref.1, s32[1,16384]{1,0:T(1,128)} %bitcast.2, s32[128,128]{1,0:T(8,128)} %bitcast.3), custom_call_target="tpu_custom_call" | custom-call | tf_op jit(solution)/shard_map/pallas_call | solution.py:470
  190.8 3.4 %shard_map.59 = (f32[64,16384]{1,0:T(8,128)}, f32[64,64]{1,0:T(8,128)}, f32[64,16384]{1,0:T(8,128)}) custom-call(f32[64,16384]{1,0:T(8,128)S(1)} %get-tuple-element.6.mixed_in, f32[64,64]{1,0:T(8,128)S(1)} %get-tuple-element.7.r_in, f32[64,16384]{1,0:T(8,128)S(1)} %get-tuple-element.8.precond_in), custom_call_target="tpu_custom_call" | custom-call | tf_op jit(solution)/shard_map/pallas_call | solution.py:503

commit v7 on v6

--- a/solution.py
+++ b/solution.py
@@ -20,7 +20,7 @@
 GROUP = 8
 CHUNKS = COLS // GROUP
 DESK, TELLER = 6, 5
-AHEAD = 4
+AHEAD = 3
 Z_LEN = COUNT // N_Z
 P_LEN = COUNT // PLANE
 INNER = 256
@@ -88,10 +88,10 @@
 
     load_signs = pltpu.make_async_copy(signs_hbm, signs_ref, signs_sem)
     load_samples = pltpu.make_async_copy(samples_hbm, samples_ref, samples_sem)
+    load_signs.start()
+    load(0).start()
     for d in range(1, N_Z):
         pl.when((z + d) % N_Z != DESK)(functools.partial(greet, [z_peers[d - 1]]))
-    load_signs.start()
-    load(0).start()
 
     @pl.when(z == TELLER)
     def _():

time: 195 us -> 195 us (level)
  no operation moved by 1% of the time
where the time goes in v7:
time: 195 us; the launch traced here: 194 us
  Pallas kernels  194 us (99%)
    pallas_call x1, Pallas kernels, body(): pl.pallas_call(functools.partial(mix_kernel, total / sample_rows.shape[0]...  190 us

profile of v7, /device:TPU:1, one launch (start us, length us, event | category | flops | bytes accessed | tf_op | source)
XLA Modules:
  0.0 194.2 jit_solution(17293473124600658642)
XLA Ops:
  0.6 190.2 %shard_map.58 = (f32[64,16384]{1,0:T(8,128)S(1)}, f32[64,64]{1,0:T(8,128)S(1)}, f32[64,16384]{1,0:T(8,128)S(1)}) custom-call(f32[64,16384]{1,0:T(8,128)} %panel_ref.1, s32[1,16384]{1,0:T(1,128)} %bitcast.2, s32[128,128]{1,0:T(8,128)} %bitcast.3), custom_call_target="tpu_custom_call" | custom-call | tf_op jit(solution)/shard_map/pallas_call | solution.py:470
  190.8 3.4 %shard_map.59 = (f32[64,16384]{1,0:T(8,128)}, f32[64,64]{1,0:T(8,128)}, f32[64,16384]{1,0:T(8,128)}) custom-call(f32[64,16384]{1,0:T(8,128)S(1)} %get-tuple-element.6.mixed_in, f32[64,64]{1,0:T(8,128)S(1)} %get-tuple-element.7.r_in, f32[64,16384]{1,0:T(8,128)S(1)} %get-tuple-element.8.precond_in), custom_call_target="tpu_custom_call" | custom-call | tf_op jit(solution)/shard_map/pallas_call | solution.py:503
